TPU v7x, 32 devices: a whole 2x2x4 slice. The times are simulated.
32 devices in a mesh: groups: 2 (over y), ctx: 4 (over z), inner: 2 (over x), chan: 2 (over core).
Axes of the slice: x: 2, y: 2, z: 4, core: 2. Of those that a mesh axis runs over, the one named last changes fastest.
Arguments:
- queries: bfloat16 [2048, 8192], P(('groups', 'ctx', 'inner'), 'chan'), parts along dimension 0, may hold values from -6 to 6
- keys_in: bfloat16 [2048, 8192], P(('groups', 'ctx', 'inner'), 'chan'), parts along dimension 0, may hold values from -6 to 6
- values_in: bfloat16 [2048, 8192], P(('groups', 'ctx', 'inner'), 'chan'), parts along dimension 0, may hold values from -6 to 6
- out_grad: bfloat16 [2048, 8192], P(('groups', 'ctx', 'inner'), 'chan'), parts along dimension 0, may hold values from -6 to 6
- short_taps: float32 [3, 7, 8192], P(None, None, 'chan'), may hold values from -2 to 2
- pole_rate: float32 [16, 512], P(None, 'chan'), may hold values from 0.0001953125 to 0.15, as said below
- residue: float32 [16, 512], P(None, 'chan'), may hold values from -0.55 to 0.55
Outputs:
- query_grad: bfloat16 [2048, 8192], P(('groups', 'ctx', 'inner'), 'chan'), parts along dimension 0
- key_grad: bfloat16 [2048, 8192], P(('groups', 'ctx', 'inner'), 'chan'), parts along dimension 0
- value_grad: bfloat16 [2048, 8192], P(('groups', 'ctx', 'inner'), 'chan'), parts along dimension 0
- tap_grad: float32 [6, 7, 8192], P('groups', None, 'chan'), parts along dimension 0
- rate_grad: float32 [32, 512], P('groups', 'chan'), parts along dimension 0
- residue_grad: float32 [32, 512], P('groups', 'chan'), parts along dimension 0
There are 2 independent parts, one for each index of `groups`. A program takes and returns all parts, laid end to end along the dimension named above; an argument that names none is the same for every part. Nothing has to cross between parts.
Inputs may be any that keep to these rules, and one draw needn't show every extreme that they name: `pole_rate`: each rate lies between 0.2 / 1024 and 0.15.
All inputs are finite; a program needn't handle non-finite values.
Results may differ from a plain program's by a relative error of at most 0.001.
Values may be sent and summed in bfloat16 or wider, within the bound.
A program may use at most 192 MiB of HBM per device.

v0:
```python
import jax
import jax.numpy as jnp
from jax import lax
from jax.sharding import PartitionSpec as P


def shifted(block, axis, distance):
    devices = range(lax.axis_size(axis))
    route = [(i - distance, i) for i in devices if i - distance in devices]
    return lax.ppermute(block, axis, route)


def carried_in_2(part, axis, combine, identity, reverse):
    count = lax.axis_size(axis)
    place = lax.axis_index(axis)
    ahead = count - 1 - place if reverse else place
    gathered = jax.tree.map(lambda a: lax.all_gather(a, axis), part)
    state = jax.tree.map(lambda a, e: jnp.zeros_like(a) + jnp.asarray(e, a.dtype), part, identity)

    def one(lap, state):
        source = count - 1 - lap if reverse else lap
        return combine(
            state, jax.tree.map(lambda a: lax.dynamic_index_in_dim(a, source, 0, False), gathered)
        )

    return lax.fori_loop(0, ahead, one, state)


def affine_join(earlier, later):
    ratio = later[0]
    carried = earlier[1]
    shape = carried.shape
    scaled = (carried.reshape(shape[0], ratio.shape[1], -1) * ratio[:, :, None]).reshape(shape)
    return (earlier[0] * ratio, scaled + later[1])


def spread(table, members):
    return jnp.repeat(table, members, axis=1)


def causal_mix(extended, taps, row_count):
    tap_count = taps.shape[0]
    running = taps[tap_count - 1] * extended[0:row_count]
    for lag_index in range(tap_count - 2, -1, -1):
        offset_row = tap_count - 1 - lag_index
        running = running + taps[lag_index] * extended[offset_row : offset_row + row_count]
    return running


def ahead_mix(extended, taps, row_count):
    tap_count = taps.shape[0]
    running = taps[0] * extended[0:row_count]
    for lag_index in range(1, tap_count):
        running = running + taps[lag_index] * extended[lag_index : lag_index + row_count]
    return running


def tap_terms(grad_mix, extended, tap_count, row_count):
    collected = []
    for lag_index in range(tap_count):
        offset_row = tap_count - 1 - lag_index
        collected.append(jnp.sum(grad_mix * extended[offset_row : offset_row + row_count], axis=0))
    return jnp.stack(collected, axis=0)


def on_device(queries, keys_in, values_in, out_grad, short_taps, pole_rate, residue):
    row_count, chan_count = queries.shape
    mode_count, local_groups = pole_rate.shape
    members = chan_count // local_groups
    tap_count = short_taps.shape[1]
    tail_rows = tap_count - 1
    devices = lax.axis_size(("ctx", "inner"))
    token_total = row_count * devices
    before = shifted(
        (
            queries[row_count - tail_rows :],
            keys_in[row_count - tail_rows :],
            values_in[row_count - tail_rows :],
        ),
        ("ctx", "inner"),
        1,
    )
    query_wide = jnp.concatenate([before[0], queries], axis=0).astype(jnp.float32)
    key_wide = jnp.concatenate([before[1], keys_in], axis=0).astype(jnp.float32)
    value_wide = jnp.concatenate([before[2], values_in], axis=0).astype(jnp.float32)
    query_mix = causal_mix(query_wide, short_taps[0], row_count)
    key_mix = causal_mix(key_wide, short_taps[1], row_count)
    value_mix = causal_mix(value_wide, short_taps[2], row_count)
    source_term = key_mix * value_mix
    grad_out = out_grad.astype(jnp.float32)
    adjoint_term = grad_out * query_mix
    lam_table = jnp.exp(-pole_rate)
    lam_rows = spread(lam_table, members)
    residue_rows = spread(residue, members)
    block_rows = 16
    block_count = row_count // block_rows
    src_blocks = source_term.reshape(block_count, block_rows, chan_count)
    adj_blocks = adjoint_term.reshape(block_count, block_rows, chan_count)
    zero_state = jnp.zeros((mode_count, chan_count), jnp.float32)

    def local_forward(state_carry, src_blk):
        following = state_carry
        for step_row in range(block_rows):
            following = lam_rows * following + src_blk[step_row]
        return (following, state_carry)

    local_final, local_starts = lax.scan(local_forward, zero_state, src_blocks)

    def local_backward(adj_carry, adj_blk):
        for step_row in range(block_rows - 1, -1, -1):
            adj_carry = lam_rows * adj_carry + adj_blk[step_row]
        return (adj_carry, None)

    local_first = lax.scan(local_backward, zero_state, adj_blocks, reverse=True)[0]
    rate_dev = pole_rate * float(row_count)
    decay_dev = jnp.exp(-rate_dev)
    neutral = (jnp.ones_like(decay_dev), jnp.zeros_like(local_final))
    state_in = carried_in_2(
        (decay_dev, local_final), ("ctx", "inner"), affine_join, neutral, False
    )[1]
    adjoint_in = carried_in_2(
        (decay_dev, local_first), ("ctx", "inner"), affine_join, neutral, True
    )[1]
    offsets = jnp.arange(block_count, dtype=jnp.float32) * float(block_rows)
    start_scale = spread(
        jnp.exp(-pole_rate[None, :, :] * offsets[:, None, None]).reshape(
            block_count * mode_count, local_groups
        ),
        members,
    ).reshape(block_count, mode_count, chan_count)
    block_starts = local_starts + start_scale * state_in[None]

    def retreat(carried_in, inputs):
        later_adj, mode_sum, rate_sum = carried_in
        src_blk, adj_blk, block_start = inputs
        states = []
        running = block_start
        out_rows = []
        for step_row in range(block_rows):
            running = lam_rows * running + src_blk[step_row]
            states.append(running)
            out_rows.append(jnp.sum(residue_rows * running, axis=0))
        adjoint = later_adj
        adj_rows = [None] * block_rows
        for step_row in range(block_rows - 1, -1, -1):
            adj_row = adj_blk[step_row]
            adjoint = lam_rows * adjoint + adj_row
            adj_rows[step_row] = jnp.sum(residue_rows * adjoint, axis=0)
            mode_sum = mode_sum + adj_row * states[step_row]
            earlier = block_start if step_row == 0 else states[step_row - 1]
            rate_sum = rate_sum + adjoint * earlier
        return (
            (adjoint, mode_sum, rate_sum),
            (jnp.stack(out_rows, axis=0), jnp.stack(adj_rows, axis=0)),
        )

    initial = (adjoint_in, zero_state, zero_state)
    carried, produced = lax.scan(
        retreat, initial, (src_blocks, adj_blocks, block_starts), reverse=True
    )
    long_out = produced[0].reshape(row_count, chan_count)
    long_adj = produced[1].reshape(row_count, chan_count)
    mode_grad = jnp.sum(carried[1].reshape(mode_count, local_groups, members), axis=2)
    rate_total = jnp.sum(carried[2].reshape(mode_count, local_groups, members), axis=2)
    pole_grad = -lam_table * residue * rate_total
    query_back = grad_out * long_out
    key_back = long_adj * value_mix
    value_back = long_adj * key_mix
    next_heads = shifted(
        (query_back[:tail_rows], key_back[:tail_rows], value_back[:tail_rows]), ("ctx", "inner"), -1
    )
    query_grad = ahead_mix(
        jnp.concatenate([query_back, next_heads[0]], axis=0), short_taps[0], row_count
    ).astype(jnp.bfloat16)
    key_grad = ahead_mix(
        jnp.concatenate([key_back, next_heads[1]], axis=0), short_taps[1], row_count
    ).astype(jnp.bfloat16)
    value_grad = ahead_mix(
        jnp.concatenate([value_back, next_heads[2]], axis=0), short_taps[2], row_count
    ).astype(jnp.bfloat16)
    tap_local = jnp.stack(
        [
            tap_terms(query_back, query_wide, tap_count, row_count),
            tap_terms(key_back, key_wide, tap_count, row_count),
            tap_terms(value_back, value_wide, tap_count, row_count),
        ],
        axis=0,
    )
    reduced = lax.psum((tap_local, mode_grad, pole_grad), ("ctx", "inner"))
    tap_grad = reduced[0] / jnp.sqrt(jnp.float32(token_total))
    residue_grad = reduced[1] / jnp.float32(token_total)
    rate_grad = reduced[2] / jnp.float32(token_total)
    return (query_grad, key_grad, value_grad, tap_grad, rate_grad, residue_grad)


def solution(mesh):
    placed = (
        P(("groups", "ctx", "inner"), "chan"),
        P(("groups", "ctx", "inner"), "chan"),
        P(("groups", "ctx", "inner"), "chan"),
        P(("groups", "ctx", "inner"), "chan"),
        P(None, None, "chan"),
        P(None, "chan"),
        P(None, "chan"),
    )
    return jax.shard_map(
        on_device,
        mesh=mesh,
        in_specs=placed,
        out_specs=(
            P(("groups", "ctx", "inner"), "chan"),
            P(("groups", "ctx", "inner"), "chan"),
            P(("groups", "ctx", "inner"), "chan"),
            P("groups", None, "chan"),
            P("groups", "chan"),
            P("groups", "chan"),
        ),
        check_vma=False,
    )
```

profile of v0, /device:TPU:0, one launch (start us, length us, event | category | flops | bytes accessed | tf_op | source)
XLA Modules:
  0.0 732.9 jit_solution(7204519826283749657)
XLA Ops:
  8.1 4.8 collective-permute-start.1
  14.4 3.4 collective-permute-start.2
  19.4 4.0 collective-permute-start
  28.6 8.5 %broadcast_in_dim.40 = f32[128,256,16]{2,1,0:T(8,128)} broadcast(f32[128,256]{1,0:T(8,128)S(1)} %fusion.109), dimensions={0,1} | broadcast | bytes 2228224 | tf_op jit(solution)/shard_map/broadcast_in_dim | solution.py:38
  37.1 15.2 %reshape_reshape.3 = f32[8,16,4096]{2,1,0:T(8,128)} reshape(f32[128,256,16]{2,1,0:T(8,128)} %broadcast_in_dim.40) | data formatting | bytes 4194304 | tf_op jit(solution)/shard_map/reshape;reshape | solution.py:130
  52.3 30.5 %all-gather = f32[128,256]{1,0:T(8,128)S(1)} all-gather(f32[16,256]{1,0:T(8,128)S(1)} %get-tuple-element.784), channel_id=2, replica_groups=mesh['groups'=2,'ctx'=4,'inner'=2,'chan'=2] {'ctx','inner'}, dimensions={0}, use_global_device_ids=true | all-gather | bytes 147456 | tf_op jit(solution)/shard_map/all_gather | solution.py:17
  86.0 4.9 fusion.110
  92.5 73.8 %while.80 = (s32[]{:T(128)}, f32[16,4096]{1,0:T(8,128)S(1)}, f32[8,16,4096]{2,1,0:T(8,128)}, f32[8,16,4096]{2,1,0:T(8,128)}, f32[16,256]{1,0:T(8,128)}, /*index=...) while((s32[]{:T(128)}, f32[16,4096]{1,0:T(8,128)S(1)}, ...), condition=%wide.region_5.6_spmd.clone, body=%wide.region_4.5_spmd.clone.sunk | while | flops 2228242 | bytes 2900932 | solution.py:107
  98.2 3.1 reshape.265
  107.6 3.1 reshape.265
  117.2 3.1 reshape.265
  126.3 3.1 reshape.265
  135.4 3.1 reshape.265
  144.5 3.1 reshape.265
  153.7 3.1 reshape.265
  162.9 3.1 reshape.265
  171.9 68.2 %while.79 = (s32[]{:T(128)}, f32[16,4096]{1,0:T(8,128)S(1)}, f32[8,16,4096]{2,1,0:T(8,128)}, f32[16,256]{1,0:T(8,128)}, s32[]{:T(128)}, /*index=5*/s32[]{:T(128)...) while((s32[]{:T(128)}, f32[16,4096]{1,0:T(8,128)S(1)}, ...), condition=%wide.region_1.2_spmd.clone, body=%wide.region_0.1_spmd.clone.sunk | while | flops 2162707 | bytes 2376143 | solution.py:114
  176.8 3.1 reshape.264
  185.4 3.1 reshape.264
  193.8 3.1 reshape.264
  202.0 3.1 reshape.264
  210.5 3.1 reshape.264
  219.1 3.1 reshape.264
  227.8 3.1 reshape.264
  236.6 3.1 reshape.264
  240.9 47.2 %all-gather.6.cloned.1.call-done = f32[128,4096]{1,0:T(8,128)} async-done(((f32[16,4096]{1,0:T(8,128)}), f32[128,4096]{1,0:T(8,128)}) %all-gather.6.cloned.1.call-update) | async-done | bytes 2097168 | tf_op jit(solution)/shard_map/all_gather | solution.py:17
  288.1 43.5 %while.77 = (s32[]{:T(128)}, f32[16,4096]{1,0:T(8,128)S(1)}, s32[]{:T(128)}, f32[8,16,256]{2,1,0:T(8,128)S(1)}, f32[8,16,4096]{2,1,0:T(8,128)}, /*index=5*/s32[]{:T(128)}, s32[]{:T(128)}, s32[]{:T(128)}, s32[]{:T(128)}) while((s32[]{:T(128)}, f32[16,4096]{1,0:T(8,128)S(1)}, s32[]{:T(128)}, f32[8,16,256]{2,1,0:T(8,128)S(1)}, ...), condition=%wide.region_3.4_spmd, body=%wide.region_2.3_spmd.sunk | while | flops 131078 | bytes 1884307 | solution.py:26
  290.1 3.1 mul.3021
  296.3 3.1 mul.3021
  302.5 3.1 mul.3021
  308.7 3.1 mul.3021
  314.9 3.1 mul.3021
  321.1 3.1 mul.3021
  327.3 3.1 mul.3021
  331.6 3.8 multiply_add_fusion.33
  338.5 290.7 %while.81 = (s32[]{:T(128)}, f32[16,4096]{1,0:T(8,128)S(1)}, f32[16,4096]{1,0:T(8,128)}, f32[16,4096]{1,0:T(8,128)}, f32[8,16,4096]{2,1,0:T(8,128)}, /*index=5*/...) while((s32[]{:T(128)}, f32[16,4096]{1,0:T(8,128)S(1)}, ...), condition=%wide.region_41.42_spmd.clone, body=%wide.region_8.41_spmd.clone.sunk | while | flops 18874388 | bytes 16942528 | solution.py:158
  343.8 3.1 reshape.267
  356.5 3.2 stack.455
  364.3 3.3 stack.454
  379.8 3.1 reshape.267
  385.6 3.1 reshape.266
  392.5 3.2 stack.455
  400.4 3.3 stack.454
  416.1 3.1 reshape.267
  421.9 3.1 reshape.266
  428.8 3.2 stack.455
  436.5 3.3 stack.454
  452.1 3.1 reshape.267
  457.9 3.1 reshape.266
  464.8 3.2 stack.455
  472.3 3.3 stack.454
  500.7 3.2 stack.455
  508.6 3.3 stack.454
  537.4 3.2 stack.455
  545.2 3.3 stack.454
  574.0 3.2 stack.455
  582.0 3.3 stack.454
  610.5 3.2 stack.455
  618.6 3.3 stack.454
  637.9 10.3 %multiply_reduce_fusion.46 = (f32[4096]{0:T(1024)S(1)}, f32[4096]{0:T(1024)S(1)}, f32[4096]{0:T(1024)S(1)}, f32[4096]{0:T(1024)S(1)}, f32[4096]{0:T(1024)S(1)}, ...) fusion(f32[134,4096]{1,0:T(8,128)} %copy-done.2, f32[8,16,4096]{2,1,0:T(8,128)} %get-tuple-element.471, ...), kind=kLoop, calls=%fused_computation.291 | loop fusion | flops 8359936 | bytes 20037632 | tf_op jit(solution)/shard_map/reduce_sum | solution.py:62
  648.3 5.7 multiply_reduce_fusion.32
  663.5 37.2 %all-reduce = (f32[16,256]{1,0:T(8,128)S(1)}, f32[16,256]{1,0:T(8,128)S(1)}) all-reduce(f32[16,256]{1,0:T(8,128)S(1)} %copy-done.86, f32[16,256]{1,0:T(8,128)S(1)} %reduce_sum.709), channel_id=1, replica_groups=mesh['groups'=2,'ctx'=4,'inner'=2,'chan'=2] {'ctx','inner'}, use_global_device_ids=true, to_apply=%region_65.66 | all-reduce | flops 8192 | bytes 65536 | tf_op jit(solution)/shard_map/psum | solution.py:189
  701.3 8.7 %fusion.59 = bf16[128,4096]{1,0:T(8,128)(2,1)} fusion(f32[6,4096]{1,0:T(8,128)S(1)} %collective-permute-done.5, f32[128,4096]{1,0:T(8,128)} %get-tuple-element.683, f32[4096]{0:T(1024)S(1)} %bitcast.601, f32[4096]{0:T(1024)S(1)} %bitcast.599, f32[4096]{0:T(1024)S(1)} %bitcast.589, f32[4096]{0:T(1024)S(1)} %bitcast.591, f32[4096]{0:T(1024)S(1)} %bitcast.593, ...), kind=kLoop, calls=%fused_computation.213 | loop fusion | flops 10485760 | bytes 3358720 | tf_op jit(solution)/shard_map/convert_element_type | solution.py:180
  716.3 7.8 %all-reduce.3.cloned.1.call-done = f32[3,7,4096]{2,1,0:T(8,128)} async-done(((f32[3,7,4096]{2,1,0:T(8,128)}), f32[3,7,4096]{2,1,0:T(8,128)}) %all-reduce.3.cloned.1.call-update) | async-done | bytes 344080 | tf_op jit(solution)/shard_map/psum | solution.py:189
  (838 shorter events, 374.0 us)
Async XLA Ops:
  7.2 233.7 %all-gather.8.cloned.1.call-start = ((), (), s32[]{:S(2)}) async-start(), calls=%async_computation.2 | async-start | bytes 2359296 | tf_op jit(solution)/shard_map/all_gather | solution.py:17
  8.1 74.7 %collective-permute-start.1 = (bf16[6,4096]{1,0:T(8,128)(2,1)S(1)}, bf16[6,4096]{1,0:T(8,128)(2,1)S(1)}, u32[]{:S(2)}, u32[]{:S(2)}) collective-permute-start(bf16[6,4096]{1,0:T(8,128)(2,1)S(1)} %slice.848), channel_id=1, source_target_pairs={{0,2},{2,4},{4,6},{6,8},{8,10},{10,12},{12,14},{1,3},{3,5},{5,7},{... | collective-permute-start | bytes 147464 | tf_op jit(solution)/shard_map/ppermute | solution.py:10
  14.4 69.9 %collective-permute-start.2 = (bf16[6,4096]{1,0:T(8,128)(2,1)}, bf16[6,4096]{1,0:T(8,128)(2,1)S(1)}, u32[]{:S(2)}, u32[]{:S(2)}) collective-permute-start(bf16[6,4096]{1,0:T(8,128)(2,1)} %slice.863), channel_id=1, source_target_pairs={{0,2},{2,4},{4,6},{6,8},{8,10},{10,12},{12,14},{1,3},{3,5},{5,7},{... | collective-permute-start | bytes 147464 | tf_op jit(solution)/shard_map/ppermute | solution.py:10
  19.4 147.9 %collective-permute-start = (bf16[6,4096]{1,0:T(8,128)(2,1)}, bf16[6,4096]{1,0:T(8,128)(2,1)}, u32[]{:S(2)}, u32[]{:S(2)}) collective-permute-start(bf16[6,4096]{1,0:T(8,128)(2,1)} %slice.834), channel_id=1, source_target_pairs={{0,2},{2,4},{4,6},{6,8},{8,10},{10,12},{12,14},{1,3},{3,5},{5,7},{... | collective-permute-start | bytes 147464 | tf_op jit(solution)/shard_map/ppermute | solution.py:10
  25.7 60.2 %copy-start.44 = (f32[1,1,4096]{2,1,0:T(1,128)}, f32[1,1,4096]{2,1,0:T(1,128)S(1)}, u32[]{:S(2)}) copy-start(f32[1,1,4096]{2,1,0:T(1,128)S(1)} %get-tuple-element.761) | copy-start | bytes 49156
  25.7 60.2 %copy-start.46 = (f32[1,1,4096]{2,1,0:T(1,128)}, f32[1,1,4096]{2,1,0:T(1,128)S(1)}, u32[]{:S(2)}) copy-start(f32[1,1,4096]{2,1,0:T(1,128)S(1)} %get-tuple-element.767) | copy-start | bytes 49156
  25.7 60.2 %copy-start.48 = (f32[1,1,4096]{2,1,0:T(1,128)}, f32[1,1,4096]{2,1,0:T(1,128)S(1)}, u32[]{:S(2)}) copy-start(f32[1,1,4096]{2,1,0:T(1,128)S(1)} %get-tuple-element.768) | copy-start | bytes 49156
  25.7 60.2 %copy-start.50 = (f32[1,1,4096]{2,1,0:T(1,128)}, f32[1,1,4096]{2,1,0:T(1,128)S(1)}, u32[]{:S(2)}) copy-start(f32[1,1,4096]{2,1,0:T(1,128)S(1)} %get-tuple-element.769) | copy-start | bytes 49156
  25.7 60.2 %copy-start.52 = (f32[1,1,4096]{2,1,0:T(1,128)}, f32[1,1,4096]{2,1,0:T(1,128)S(1)}, u32[]{:S(2)}) copy-start(f32[1,1,4096]{2,1,0:T(1,128)S(1)} %get-tuple-element.770) | copy-start | bytes 49156
  25.8 60.2 %copy-start.54 = (f32[1,1,4096]{2,1,0:T(1,128)}, f32[1,1,4096]{2,1,0:T(1,128)S(1)}, u32[]{:S(2)}) copy-start(f32[1,1,4096]{2,1,0:T(1,128)S(1)} %get-tuple-element.771) | copy-start | bytes 49156
  25.8 60.2 %copy-start.56 = (f32[1,1,4096]{2,1,0:T(1,128)}, f32[1,1,4096]{2,1,0:T(1,128)S(1)}, u32[]{:S(2)}) copy-start(f32[1,1,4096]{2,1,0:T(1,128)S(1)} %get-tuple-element.772) | copy-start | bytes 49156
  25.8 60.2 %copy-start.58 = (f32[1,1,4096]{2,1,0:T(1,128)}, f32[1,1,4096]{2,1,0:T(1,128)S(1)}, u32[]{:S(2)}) copy-start(f32[1,1,4096]{2,1,0:T(1,128)S(1)} %get-tuple-element.762) | copy-start | bytes 49156
  25.8 60.2 %copy-start.60 = (f32[1,1,4096]{2,1,0:T(1,128)}, f32[1,1,4096]{2,1,0:T(1,128)S(1)}, u32[]{:S(2)}) copy-start(f32[1,1,4096]{2,1,0:T(1,128)S(1)} %get-tuple-element.763) | copy-start | bytes 49156
  25.8 60.2 %copy-start.62 = (f32[1,1,4096]{2,1,0:T(1,128)}, f32[1,1,4096]{2,1,0:T(1,128)S(1)}, u32[]{:S(2)}) copy-start(f32[1,1,4096]{2,1,0:T(1,128)S(1)} %get-tuple-element.764) | copy-start | bytes 49156
  25.8 60.2 %copy-start.64 = (f32[1,1,4096]{2,1,0:T(1,128)}, f32[1,1,4096]{2,1,0:T(1,128)S(1)}, u32[]{:S(2)}) copy-start(f32[1,1,4096]{2,1,0:T(1,128)S(1)} %get-tuple-element.765) | copy-start | bytes 49156
  25.8 60.2 %copy-start.66 = (f32[1,1,4096]{2,1,0:T(1,128)}, f32[1,1,4096]{2,1,0:T(1,128)S(1)}, u32[]{:S(2)}) copy-start(f32[1,1,4096]{2,1,0:T(1,128)S(1)} %get-tuple-element.766) | copy-start | bytes 49156
  25.8 143.1 %copy-start.72 = (f32[1,1,4096]{2,1,0:T(1,128)}, f32[1,1,4096]{2,1,0:T(1,128)S(1)}, u32[]{:S(2)}) copy-start(f32[1,1,4096]{2,1,0:T(1,128)S(1)} %get-tuple-element.773) | copy-start | bytes 49156
  25.8 143.1 %copy-start.74 = (f32[1,1,4096]{2,1,0:T(1,128)}, f32[1,1,4096]{2,1,0:T(1,128)S(1)}, u32[]{:S(2)}) copy-start(f32[1,1,4096]{2,1,0:T(1,128)S(1)} %get-tuple-element.774) | copy-start | bytes 49156
  25.8 143.1 %copy-start.76 = (f32[1,1,4096]{2,1,0:T(1,128)}, f32[1,1,4096]{2,1,0:T(1,128)S(1)}, u32[]{:S(2)}) copy-start(f32[1,1,4096]{2,1,0:T(1,128)S(1)} %get-tuple-element.775) | copy-start | bytes 49156
  25.9 143.1 %copy-start.78 = (f32[1,1,4096]{2,1,0:T(1,128)}, f32[1,1,4096]{2,1,0:T(1,128)S(1)}, u32[]{:S(2)}) copy-start(f32[1,1,4096]{2,1,0:T(1,128)S(1)} %get-tuple-element.776) | copy-start | bytes 49156
  25.9 143.1 %copy-start.80 = (f32[1,1,4096]{2,1,0:T(1,128)}, f32[1,1,4096]{2,1,0:T(1,128)S(1)}, u32[]{:S(2)}) copy-start(f32[1,1,4096]{2,1,0:T(1,128)S(1)} %get-tuple-element.777) | copy-start | bytes 49156
  25.9 143.1 %copy-start.82 = (f32[1,1,4096]{2,1,0:T(1,128)}, f32[1,1,4096]{2,1,0:T(1,128)S(1)}, u32[]{:S(2)}) copy-start(f32[1,1,4096]{2,1,0:T(1,128)S(1)} %get-tuple-element.778) | copy-start | bytes 49156
  25.9 143.1 %copy-start.84 = (f32[1,1,4096]{2,1,0:T(1,128)}, f32[1,1,4096]{2,1,0:T(1,128)S(1)}, u32[]{:S(2)}) copy-start(f32[1,1,4096]{2,1,0:T(1,128)S(1)} %get-tuple-element.779) | copy-start | bytes 49156
  26.9 59.1 %copy-start.68 = (f32[1,1,4096]{2,1,0:T(1,128)}, f32[1,1,4096]{2,1,0:T(1,128)S(1)}, u32[]{:S(2)}) copy-start(f32[1,1,4096]{2,1,0:T(1,128)S(1)} %get-tuple-element.780) | copy-start | bytes 49156
  26.9 59.1 %copy-start.70 = (f32[1,1,4096]{2,1,0:T(1,128)}, f32[1,1,4096]{2,1,0:T(1,128)S(1)}, u32[]{:S(2)}) copy-start(f32[1,1,4096]{2,1,0:T(1,128)S(1)} %get-tuple-element.781) | copy-start | bytes 49156
  167.0 121.0 %all-gather.6.cloned.1.call-start = ((), (), s32[]{:S(2)}) async-start(), calls=%async_computation.1 | async-start | bytes 2359296 | tf_op jit(solution)/shard_map/all_gather | solution.py:17
  240.8 483.3 %all-reduce.3.cloned.1.call-start = ((), (), s32[]{:S(2)}) async-start(), calls=%async_computation | async-start | bytes 786432 | tf_op jit(solution)/shard_map/psum | solution.py:189
  341.1 14.1 %copy-start.5 = (f32[1,1,4096]{2,1,0:T(1,128)}, f32[1,1,4096]{2,1,0:T(1,128)S(1)}, u32[]{:S(2)}) copy-start(f32[1,1,4096]{2,1,0:T(1,128)S(1)} %get-tuple-element.1135) | copy-start | bytes 49156 | tf_op jit(solution)/shard_map/while
  341.1 14.1 %copy-start.6 = (f32[1,1,4096]{2,1,0:T(1,128)}, f32[1,1,4096]{2,1,0:T(1,128)S(1)}, u32[]{:S(2)}) copy-start(f32[1,1,4096]{2,1,0:T(1,128)S(1)} %get-tuple-element.1136) | copy-start | bytes 49156 | tf_op jit(solution)/shard_map/while
  341.1 14.1 %copy-start.7 = (f32[1,1,4096]{2,1,0:T(1,128)}, f32[1,1,4096]{2,1,0:T(1,128)S(1)}, u32[]{:S(2)}) copy-start(f32[1,1,4096]{2,1,0:T(1,128)S(1)} %get-tuple-element.1137) | copy-start | bytes 49156 | tf_op jit(solution)/shard_map/while
  377.1 14.1 %copy-start.5 = (f32[1,1,4096]{2,1,0:T(1,128)}, f32[1,1,4096]{2,1,0:T(1,128)S(1)}, u32[]{:S(2)}) copy-start(f32[1,1,4096]{2,1,0:T(1,128)S(1)} %get-tuple-element.1135) | copy-start | bytes 49156 | tf_op jit(solution)/shard_map/while
  377.2 14.1 %copy-start.6 = (f32[1,1,4096]{2,1,0:T(1,128)}, f32[1,1,4096]{2,1,0:T(1,128)S(1)}, u32[]{:S(2)}) copy-start(f32[1,1,4096]{2,1,0:T(1,128)S(1)} %get-tuple-element.1136) | copy-start | bytes 49156 | tf_op jit(solution)/shard_map/while
  377.2 14.1 %copy-start.7 = (f32[1,1,4096]{2,1,0:T(1,128)}, f32[1,1,4096]{2,1,0:T(1,128)S(1)}, u32[]{:S(2)}) copy-start(f32[1,1,4096]{2,1,0:T(1,128)S(1)} %get-tuple-element.1137) | copy-start | bytes 49156 | tf_op jit(solution)/shard_map/while
  413.4 14.1 %copy-start.5 = (f32[1,1,4096]{2,1,0:T(1,128)}, f32[1,1,4096]{2,1,0:T(1,128)S(1)}, u32[]{:S(2)}) copy-start(f32[1,1,4096]{2,1,0:T(1,128)S(1)} %get-tuple-element.1135) | copy-start | bytes 49156 | tf_op jit(solution)/shard_map/while
  413.4 14.1 %copy-start.6 = (f32[1,1,4096]{2,1,0:T(1,128)}, f32[1,1,4096]{2,1,0:T(1,128)S(1)}, u32[]{:S(2)}) copy-start(f32[1,1,4096]{2,1,0:T(1,128)S(1)} %get-tuple-element.1136) | copy-start | bytes 49156 | tf_op jit(solution)/shard_map/while
  413.4 14.1 %copy-start.7 = (f32[1,1,4096]{2,1,0:T(1,128)}, f32[1,1,4096]{2,1,0:T(1,128)S(1)}, u32[]{:S(2)}) copy-start(f32[1,1,4096]{2,1,0:T(1,128)S(1)} %get-tuple-element.1137) | copy-start | bytes 49156 | tf_op jit(solution)/shard_map/while
  449.4 14.1 %copy-start.5 = (f32[1,1,4096]{2,1,0:T(1,128)}, f32[1,1,4096]{2,1,0:T(1,128)S(1)}, u32[]{:S(2)}) copy-start(f32[1,1,4096]{2,1,0:T(1,128)S(1)} %get-tuple-element.1135) | copy-start | bytes 49156 | tf_op jit(solution)/shard_map/while
  449.4 14.1 %copy-start.6 = (f32[1,1,4096]{2,1,0:T(1,128)}, f32[1,1,4096]{2,1,0:T(1,128)S(1)}, u32[]{:S(2)}) copy-start(f32[1,1,4096]{2,1,0:T(1,128)S(1)} %get-tuple-element.1136) | copy-start | bytes 49156 | tf_op jit(solution)/shard_map/while
  485.3 14.1 %copy-start.5 = (f32[1,1,4096]{2,1,0:T(1,128)}, f32[1,1,4096]{2,1,0:T(1,128)S(1)}, u32[]{:S(2)}) copy-start(f32[1,1,4096]{2,1,0:T(1,128)S(1)} %get-tuple-element.1135) | copy-start | bytes 49156 | tf_op jit(solution)/shard_map/while
  485.4 14.1 %copy-start.6 = (f32[1,1,4096]{2,1,0:T(1,128)}, f32[1,1,4096]{2,1,0:T(1,128)S(1)}, u32[]{:S(2)}) copy-start(f32[1,1,4096]{2,1,0:T(1,128)S(1)} %get-tuple-element.1136) | copy-start | bytes 49156 | tf_op jit(solution)/shard_map/while
  522.0 14.1 %copy-start.5 = (f32[1,1,4096]{2,1,0:T(1,128)}, f32[1,1,4096]{2,1,0:T(1,128)S(1)}, u32[]{:S(2)}) copy-start(f32[1,1,4096]{2,1,0:T(1,128)S(1)} %get-tuple-element.1135) | copy-start | bytes 49156 | tf_op jit(solution)/shard_map/while
  522.0 14.1 %copy-start.6 = (f32[1,1,4096]{2,1,0:T(1,128)}, f32[1,1,4096]{2,1,0:T(1,128)S(1)}, u32[]{:S(2)}) copy-start(f32[1,1,4096]{2,1,0:T(1,128)S(1)} %get-tuple-element.1136) | copy-start | bytes 49156 | tf_op jit(solution)/shard_map/while
  558.6 14.1 %copy-start.5 = (f32[1,1,4096]{2,1,0:T(1,128)}, f32[1,1,4096]{2,1,0:T(1,128)S(1)}, u32[]{:S(2)}) copy-start(f32[1,1,4096]{2,1,0:T(1,128)S(1)} %get-tuple-element.1135) | copy-start | bytes 49156 | tf_op jit(solution)/shard_map/while
  558.6 14.1 %copy-start.6 = (f32[1,1,4096]{2,1,0:T(1,128)}, f32[1,1,4096]{2,1,0:T(1,128)S(1)}, u32[]{:S(2)}) copy-start(f32[1,1,4096]{2,1,0:T(1,128)S(1)} %get-tuple-element.1136) | copy-start | bytes 49156 | tf_op jit(solution)/shard_map/while
  558.6 14.1 %copy-start.7 = (f32[1,1,4096]{2,1,0:T(1,128)}, f32[1,1,4096]{2,1,0:T(1,128)S(1)}, u32[]{:S(2)}) copy-start(f32[1,1,4096]{2,1,0:T(1,128)S(1)} %get-tuple-element.1137) | copy-start | bytes 49156 | tf_op jit(solution)/shard_map/while
  595.1 14.1 %copy-start.5 = (f32[1,1,4096]{2,1,0:T(1,128)}, f32[1,1,4096]{2,1,0:T(1,128)S(1)}, u32[]{:S(2)}) copy-start(f32[1,1,4096]{2,1,0:T(1,128)S(1)} %get-tuple-element.1135) | copy-start | bytes 49156 | tf_op jit(solution)/shard_map/while
  595.1 14.1 %copy-start.6 = (f32[1,1,4096]{2,1,0:T(1,128)}, f32[1,1,4096]{2,1,0:T(1,128)S(1)}, u32[]{:S(2)}) copy-start(f32[1,1,4096]{2,1,0:T(1,128)S(1)} %get-tuple-element.1136) | copy-start | bytes 49156 | tf_op jit(solution)/shard_map/while
  654.6 46.7 %copy-start.59 = (f32[1,1,4096]{2,1,0:T(1,128)S(1)}, f32[1,1,4096]{2,1,0:T(1,128)}, u32[]{:S(2)}) copy-start(f32[1,1,4096]{2,1,0:T(1,128)} %copy-done.58) | copy-start | bytes 49156
  654.6 46.7 %copy-start.61 = (f32[1,1,4096]{2,1,0:T(1,128)S(1)}, f32[1,1,4096]{2,1,0:T(1,128)}, u32[]{:S(2)}) copy-start(f32[1,1,4096]{2,1,0:T(1,128)} %copy-done.60) | copy-start | bytes 49156
  654.6 46.7 %copy-start.63 = (f32[1,1,4096]{2,1,0:T(1,128)S(1)}, f32[1,1,4096]{2,1,0:T(1,128)}, u32[]{:S(2)}) copy-start(f32[1,1,4096]{2,1,0:T(1,128)} %copy-done.62) | copy-start | bytes 49156
  654.6 46.7 %copy-start.65 = (f32[1,1,4096]{2,1,0:T(1,128)S(1)}, f32[1,1,4096]{2,1,0:T(1,128)}, u32[]{:S(2)}) copy-start(f32[1,1,4096]{2,1,0:T(1,128)} %copy-done.64) | copy-start | bytes 49156
  654.6 46.7 %copy-start.67 = (f32[1,1,4096]{2,1,0:T(1,128)S(1)}, f32[1,1,4096]{2,1,0:T(1,128)}, u32[]{:S(2)}) copy-start(f32[1,1,4096]{2,1,0:T(1,128)} %copy-done.66) | copy-start | bytes 49156
  654.6 46.7 %copy-start.69 = (f32[1,1,4096]{2,1,0:T(1,128)S(1)}, f32[1,1,4096]{2,1,0:T(1,128)}, u32[]{:S(2)}) copy-start(f32[1,1,4096]{2,1,0:T(1,128)} %copy-done.68) | copy-start | bytes 49156
  654.6 46.7 %copy-start.71 = (f32[1,1,4096]{2,1,0:T(1,128)S(1)}, f32[1,1,4096]{2,1,0:T(1,128)}, u32[]{:S(2)}) copy-start(f32[1,1,4096]{2,1,0:T(1,128)} %copy-done.70) | copy-start | bytes 49156
  656.3 44.9 %collective-permute-start.5 = (f32[6,4096]{1,0:T(8,128)S(1)}, f32[6,4096]{1,0:T(8,128)S(1)}, u32[]{:S(2)}, u32[]{:S(2)}) collective-permute-start(f32[6,4096]{1,0:T(8,128)S(1)} %slice.1005), channel_id=1, source_target_pairs={{2,0},{4,2},{6,4},{8,6},{10,8},{12,10},{14,12},{3,1},{5,3},{7,5},{... | collective-permute-start | bytes 294920 | tf_op jit(solution)/shard_map/ppermute | solution.py:10
  657.7 52.5 %collective-permute-start.4 = (f32[6,4096]{1,0:T(8,128)S(1)}, f32[6,4096]{1,0:T(8,128)S(1)}, u32[]{:S(2)}, u32[]{:S(2)}) collective-permute-start(f32[6,4096]{1,0:T(8,128)S(1)} %slice.994), channel_id=1, source_target_pairs={{2,0},{4,2},{6,4},{8,6},{10,8},{12,10},{14,12},{3,1},{5,3},{7,5},{... | collective-permute-start | bytes 294920 | tf_op jit(solution)/shard_map/ppermute | solution.py:10
  659.9 53.4 %collective-permute-start.3 = (f32[6,4096]{1,0:T(8,128)S(1)}, f32[6,4096]{1,0:T(8,128)S(1)}, u32[]{:S(2)}, u32[]{:S(2)}) collective-permute-start(f32[6,4096]{1,0:T(8,128)S(1)} %slice.983), channel_id=1, source_target_pairs={{2,0},{4,2},{6,4},{8,6},{10,8},{12,10},{14,12},{3,1},{5,3},{7,5},{... | collective-permute-start | bytes 294920 | tf_op jit(solution)/shard_map/ppermute | solution.py:10
  663.4 46.7 %copy-start.45 = (f32[1,1,4096]{2,1,0:T(1,128)S(1)}, f32[1,1,4096]{2,1,0:T(1,128)}, u32[]{:S(2)}) copy-start(f32[1,1,4096]{2,1,0:T(1,128)} %copy-done.44) | copy-start | bytes 49156
  663.4 46.7 %copy-start.47 = (f32[1,1,4096]{2,1,0:T(1,128)S(1)}, f32[1,1,4096]{2,1,0:T(1,128)}, u32[]{:S(2)}) copy-start(f32[1,1,4096]{2,1,0:T(1,128)} %copy-done.46) | copy-start | bytes 49156
  663.4 46.7 %copy-start.49 = (f32[1,1,4096]{2,1,0:T(1,128)S(1)}, f32[1,1,4096]{2,1,0:T(1,128)}, u32[]{:S(2)}) copy-start(f32[1,1,4096]{2,1,0:T(1,128)} %copy-done.48) | copy-start | bytes 49156
  663.4 46.7 %copy-start.51 = (f32[1,1,4096]{2,1,0:T(1,128)S(1)}, f32[1,1,4096]{2,1,0:T(1,128)}, u32[]{:S(2)}) copy-start(f32[1,1,4096]{2,1,0:T(1,128)} %copy-done.50) | copy-start | bytes 49156
  663.4 46.7 %copy-start.53 = (f32[1,1,4096]{2,1,0:T(1,128)S(1)}, f32[1,1,4096]{2,1,0:T(1,128)}, u32[]{:S(2)}) copy-start(f32[1,1,4096]{2,1,0:T(1,128)} %copy-done.52) | copy-start | bytes 49156
  663.5 46.7 %copy-start.55 = (f32[1,1,4096]{2,1,0:T(1,128)S(1)}, f32[1,1,4096]{2,1,0:T(1,128)}, u32[]{:S(2)}) copy-start(f32[1,1,4096]{2,1,0:T(1,128)} %copy-done.54) | copy-start | bytes 49156
  663.5 46.7 %copy-start.57 = (f32[1,1,4096]{2,1,0:T(1,128)S(1)}, f32[1,1,4096]{2,1,0:T(1,128)}, u32[]{:S(2)}) copy-start(f32[1,1,4096]{2,1,0:T(1,128)} %copy-done.56) | copy-start | bytes 49156
  (249 other events, 1540.4 us)
Sparse Core Ops, SparseCore 0:
  167.2 47.0 all-gather.7
  240.9 47.1 all-gather.5
  655.6 68.5 all-reduce.2
where the time goes:
time: 747 us; the launch traced here: 733 us
  local copies, waits for them, and re-layouts  411 us (55%)
  other arithmetic  163 us (22%)
  blocking collectives  67.7 us (9%)
  waiting for transfers between devices  55 us (7%)
  starting transfers between devices  16.5 us (2%)
  between operations  15.2 us (2%)
    reshape x32, local copies, waits for them, and re-layouts, spread(): return jnp.repeat(table, members, axis=1)  101 us
    broadcast_in_dim x33, local copies, waits for them, and re-layouts, spread(): return jnp.repeat(table, members, axis=1)  92.8 us
    all_gather x2, waiting for transfers between devices, carried_in_2(): gathered = jax.tree.map(lambda a: lax.all_gather(a, axis), part)  47.2 us
    psum x1, blocking collectives, on_device(): reduced = lax.psum((tap_local, mode_grad, pole_grad), ('ctx', 'inner'))  37.2 us
    mul x21, local copies, waits for them, and re-layouts, affine_join(): carried.reshape(shape[0], ratio.shape[1], -1) * ratio[:, :, None]  35.7 us
    all_gather x1, blocking collectives, carried_in_2(): gathered = jax.tree.map(lambda a: lax.all_gather(a, axis), part)  30.5 us
    reduce_sum x16, other arithmetic, retreat(): out_rows.append(jnp.sum(residue_rows * running, axis=0))  29.3 us
    another operation x8, local copies, waits for them, and re-layouts, retreat(): jnp.stack(adj_rows, axis=0)  26.7 us
  transfers between devices with their start and end apart: 9, of which 2 were waited for; matrix products, arithmetic and copies ran while one was open for 28% of the time, Pallas kernels for 0%

commit v1 on v0

v1 whole, which is shorter than its diff:
```python
import functools

import jax
import jax.numpy as jnp
from jax import lax
from jax.experimental import pallas as pl
from jax.experimental.pallas import tpu as pltpu
from jax.sharding import PartitionSpec as P

LINE = ("ctx", "inner")
LANES = 128
SUB = 8
EXACT = lax.Precision.HIGHEST


def moved(block, distance):
    devices = range(lax.axis_size(LINE))
    return lax.ppermute(block, LINE, [(i, i + distance) for i in devices if i + distance in devices])


def carried_in(total, decay, reverse):
    sign = -1 if reverse else 1
    count = lax.axis_size(LINE)
    state = moved(total, sign)
    distance = 1
    while distance < count - 1:
        state = state + decay * moved(state, sign * distance)
        decay = decay * decay
        distance *= 2
    return state


def summed(block):
    count = lax.axis_size(LINE)
    distance = 1
    while distance < count:
        block = block + lax.ppermute(block, LINE, [(i, i ^ distance) for i in range(count)])
        distance *= 2
    return block


def spread_matrix(local_groups, width, members):
    first = pl.program_id(0) * width
    row = lax.broadcasted_iota(jnp.int32, (local_groups, width), 0)
    col = lax.broadcasted_iota(jnp.int32, (local_groups, width), 1) + first
    low = row * members
    return jnp.where((col >= low) & (col < low + members), 1.0, 0.0).astype(jnp.float32)


def first_kernel(members, q_ref, k_ref, v_ref, g_ref, prev_ref, next_ref, taps_ref, rate_ref, res_ref,
                 mix_ref, ef_ref, ea_ref, final_ref, first_ref, rates_ref, ress_ref, wide, src, adj, each):
    rows, width = q_ref.shape
    modes, local_groups = rate_ref.shape
    tap_count = taps_ref.shape[1]
    steps = rows // SUB
    onto = spread_matrix(local_groups, width, members)
    rates_ref[...] = jnp.dot(rate_ref[...], onto, precision=EXACT, preferred_element_type=jnp.float32)
    ress_ref[...] = jnp.dot(res_ref[...], onto, precision=EXACT, preferred_element_type=jnp.float32)
    for i, x_ref in enumerate((q_ref, k_ref, v_ref)):
        wide[i, 0:SUB] = prev_ref[i]
        wide[i, SUB:SUB + rows] = x_ref[...].astype(jnp.float32)
        wide[i, SUB + rows:] = next_ref[i]
    chunk = lax.broadcasted_iota(jnp.int32, (SUB, LANES), 0).astype(jnp.float32)

    @pl.loop(0, width // LANES)
    def _(column):
        cols = pl.ds(pl.multiple_of(column * LANES, LANES), LANES)
        mixes = []
        for i in range(3):
            total = taps_ref[i, 0:1, cols] * wide[i, SUB:, cols]
            for j in range(1, tap_count):
                total = total + taps_ref[i, j:j + 1, cols] * wide[i, SUB - j:2 * SUB + rows - j, cols]
            mix_ref[i, :, cols] = total
            mixes.append(total[:rows])
        src[:, :] = mixes[1] * mixes[2]
        adj[:, :] = mixes[0] * g_ref[:, cols].astype(jnp.float32)
        s = [src[pl.ds(j, SUB, stride=steps), :] for j in range(steps)]
        a = [adj[pl.ds(j, SUB, stride=steps), :] for j in range(steps)]

        for n in range(modes):
            each[0, n] = jnp.broadcast_to(rates_ref[n:n + 1, cols], (SUB, LANES))

        def one(n, nothing):
            rate = each[0, n]
            lam = jnp.exp(-rate)
            ahead = s[0]
            back = a[steps - 1]
            for j in range(1, steps):
                ahead = lam * ahead + s[j]
                back = lam * back + a[steps - 1 - j]
            ef_ref[n, :, cols] = ahead
            ea_ref[n, :, cols] = back
            later = jnp.exp(rate * ((chunk - (SUB - 1)) * float(steps)))
            sooner = jnp.exp(rate * (chunk * -float(steps)))
            each[1, n] = ahead * later
            each[2, n] = back * sooner
            return nothing

        lax.fori_loop(0, modes, one, 0, unroll=4)
        final_ref[:, cols] = jnp.sum(each[1], axis=1)
        first_ref[:, cols] = jnp.sum(each[2], axis=1)


def second_kernel(members, q_ref, k_ref, v_ref, g_ref, prev_ref, gnext_ref, taps_ref, mix_ref, ef_ref, ea_ref,
                  final_ref, rates_ref, ress_ref, sin_ref, pin_ref,
                  qg_ref, kg_ref, vg_ref, tap_ref, mode_ref, pole_ref,
                  wide, src, adj, long_out, long_adj, back, mode_rows, pole_rows, each):
    rows, width = q_ref.shape
    modes = rates_ref.shape[0]
    local_groups = mode_ref.shape[1]
    tap_count = taps_ref.shape[1]
    steps = rows // SUB
    for i, x_ref in enumerate((q_ref, k_ref, v_ref)):
        wide[i, 0:SUB] = prev_ref[i]
        wide[i, SUB:] = x_ref[...].astype(jnp.float32)
    chunk = lax.broadcasted_iota(jnp.int32, (SUB, LANES), 0)

    @pl.loop(0, width // LANES)
    def _(column):
        cols = pl.ds(pl.multiple_of(column * LANES, LANES), LANES)
        src[:, :] = mix_ref[1, :, cols] * mix_ref[2, :, cols]
        adj[:rows, :] = mix_ref[0, :rows, cols] * g_ref[:, cols].astype(jnp.float32)
        adj[rows:, :] = mix_ref[0, rows:, cols] * gnext_ref[:, cols]
        s = [src[pl.ds(j, SUB, stride=steps), :] for j in range(steps)]
        a = [adj[pl.ds(j, SUB, stride=steps), :] for j in range(steps)]
        zero = jnp.zeros((SUB, LANES), jnp.float32)

        lam_table = jnp.exp(-rates_ref[:, cols])
        decay_table = jnp.exp(rates_ref[:, cols] * -float(steps))
        tables = (lam_table, ress_ref[:, cols], decay_table, sin_ref[:, cols], pin_ref[:, cols])
        for i, table in enumerate(tables):
            for n in range(modes):
                each[i, n] = jnp.broadcast_to(table[n:n + 1], (SUB, LANES))

        def one(n, sums):
            outs, adjs = list(sums[0]), list(sums[1])
            lam, res, decay = each[0, n], each[1, n], each[2, n]
            state = jnp.where(chunk == 0, each[3, n], pltpu.roll(ef_ref[n, :, cols], 1, 0))
            late = jnp.where(chunk == SUB - 1, each[4, n], pltpu.roll(ea_ref[n, :, cols], SUB - 1, 0))
            distance = 1
            while distance < SUB:
                state = state + jnp.where(chunk >= distance, decay * pltpu.roll(state, distance, 0), 0.0)
                late = late + jnp.where(chunk < SUB - distance, decay * pltpu.roll(late, SUB - distance, 0), 0.0)
                decay = decay * decay
                distance *= 2
            states = [state]
            mode_sum = zero
            for j in range(steps):
                state = lam * state + s[j]
                states.append(state)
                outs[j] = outs[j] + res * state
                mode_sum = mode_sum + a[j] * state
            pole_sum = zero
            for j in range(steps - 1, -1, -1):
                late = lam * late + a[j]
                adjs[j] = adjs[j] + res * late
                pole_sum = pole_sum + late * states[j]
            each[5, n] = mode_sum
            each[6, n] = lam * res * pole_sum
            return tuple(outs), tuple(adjs)

        outs, adjs = lax.fori_loop(0, modes, one, ((zero,) * steps, (zero,) * steps))
        mode_rows[:, cols] = jnp.sum(each[5], axis=1)
        pole_rows[:, cols] = jnp.sum(each[6], axis=1)
        for j in range(steps):
            long_out[pl.ds(j, SUB, stride=steps), :] = outs[j]
            long_adj[pl.ds(j, SUB, stride=steps), :] = adjs[j]
        rate = rates_ref[:, cols]
        res = ress_ref[:, cols]
        lam = jnp.exp(-rate)
        grow = jnp.exp(rate)
        state = jnp.exp(rate * -float(rows)) * sin_ref[:, cols] + final_ref[:, cols]
        late = pin_ref[:, cols]
        long_out[rows:, :] = zero
        long_adj[rows:, :] = zero
        for j in range(tap_count - 1):
            state = lam * state + src[rows + j:rows + j + 1, :]
            long_out[rows + j:rows + j + 1, :] = jnp.sum(res * state, axis=0, keepdims=True)
            long_adj[rows + j:rows + j + 1, :] = jnp.sum(res * late, axis=0, keepdims=True)
            late = (late - adj[rows + j:rows + j + 1, :]) * grow
        back[0, :rows, cols] = g_ref[:, cols].astype(jnp.float32) * long_out[:rows, :]
        back[0, rows:, cols] = gnext_ref[:, cols] * long_out[rows:, :]
        back[1, :, cols] = long_adj[:, :] * mix_ref[2, :, cols]
        back[2, :, cols] = long_adj[:, :] * mix_ref[1, :, cols]
        for i, grad_ref in enumerate((qg_ref, kg_ref, vg_ref)):
            mine = back[i, 0:rows, cols]
            total = taps_ref[i, 0:1, cols] * mine
            for j in range(1, tap_count):
                total = total + taps_ref[i, j:j + 1, cols] * back[i, j:j + rows, cols]
            grad_ref[:, cols] = total.astype(grad_ref.dtype)
            for j in range(tap_count):
                tap_ref[i, j:j + 1, cols] = jnp.sum(
                    mine * wide[i, SUB - j:SUB - j + rows, cols], axis=0, keepdims=True
                )
            for j in range(tap_count, SUB):
                tap_ref[i, j:j + 1, cols] = jnp.zeros((1, LANES), jnp.float32)

    onto = spread_matrix(local_groups, width, members)
    along = (((1,), (1,)), ((), ()))

    @pl.when(pl.program_id(0) == 0)
    def _():
        mode_ref[...] = jnp.zeros_like(mode_ref)
        pole_ref[...] = jnp.zeros_like(pole_ref)

    mode_ref[...] += lax.dot_general(
        mode_rows[...], onto, along, precision=EXACT, preferred_element_type=jnp.float32
    )
    pole_ref[...] += lax.dot_general(
        pole_rows[...], onto, along, precision=EXACT, preferred_element_type=jnp.float32
    )


def on_device(queries, keys_in, values_in, out_grad, short_taps, pole_rate, residue):
    rows, chans = queries.shape
    modes, local_groups = pole_rate.shape
    members = chans // local_groups
    tap_count = short_taps.shape[1]
    token_total = rows * lax.axis_size(LINE)
    width = min(512, chans)
    f32 = jnp.float32
    tails = jnp.stack([x[rows - SUB:] for x in (queries, keys_in, values_in)])
    heads = jnp.stack([x[:SUB] for x in (queries, keys_in, values_in, out_grad)])
    before = moved(tails, 1).astype(f32)
    after = moved(heads, -1).astype(f32)

    def cut(*lead):
        zeros = (0,) * len(lead)
        return pl.BlockSpec((*lead, width), lambda i: (*zeros, i))

    def full(*shape):
        zeros = (0,) * len(shape)
        return pl.BlockSpec(shape, lambda i: zeros)

    def arr(*shape, dtype=f32):
        return jax.ShapeDtypeStruct(shape, dtype)

    params = pltpu.CompilerParams(vmem_limit_bytes=48 * 1024 * 1024)
    wide_rows = rows + SUB
    streams = [cut(rows)] * 4
    mix, ef, ea, final, first, rates, ress = pl.pallas_call(
        functools.partial(first_kernel, members),
        grid=(chans // width,),
        in_specs=streams + [
            cut(3, SUB), cut(3, SUB), cut(3, tap_count), full(modes, local_groups), full(modes, local_groups)
        ],
        out_specs=[cut(3, wide_rows), cut(modes, SUB), cut(modes, SUB)] + [cut(modes)] * 4,
        out_shape=[arr(3, wide_rows, chans), arr(modes, SUB, chans), arr(modes, SUB, chans)]
        + [arr(modes, chans)] * 4,
        scratch_shapes=[
            pltpu.VMEM((3, wide_rows + SUB, width), f32),
            pltpu.VMEM((rows, LANES), f32),
            pltpu.VMEM((rows, LANES), f32),
            pltpu.VMEM((3, modes, SUB, LANES), f32),
        ],
        compiler_params=params,
        name="local_states",
    )(queries, keys_in, values_in, out_grad, before, after[:3], short_taps, pole_rate, residue)
    decay = jnp.exp(rates * -float(rows))
    state_in = carried_in(final, decay, False)
    late_in = carried_in(first, decay, True)
    query_grad, key_grad, value_grad, taps_sum, mode_sum, pole_sum = pl.pallas_call(
        functools.partial(second_kernel, members),
        grid=(chans // width,),
        in_specs=streams + [
            cut(3, SUB), cut(SUB), cut(3, tap_count), cut(3, wide_rows), cut(modes, SUB), cut(modes, SUB)
        ] + [cut(modes)] * 5,
        out_specs=[cut(rows)] * 3 + [cut(3, SUB), full(modes, local_groups), full(modes, local_groups)],
        out_shape=[arr(rows, chans, dtype=jnp.bfloat16)] * 3
        + [arr(3, SUB, chans), arr(modes, local_groups), arr(modes, local_groups)],
        scratch_shapes=[pltpu.VMEM((3, wide_rows, width), f32)]
        + [pltpu.VMEM((wide_rows, LANES), f32)] * 4
        + [pltpu.VMEM((3, wide_rows, width), f32)]
        + [pltpu.VMEM((modes, width), f32)] * 2
        + [pltpu.VMEM((7, modes, SUB, LANES), f32)],
        compiler_params=params,
        name="gradients",
    )(queries, keys_in, values_in, out_grad, before, after[3], short_taps, mix, ef, ea,
      final, rates, ress, state_in, late_in)
    taps_sum, mode_sum, pole_sum = summed_all(taps_sum, mode_sum, pole_sum)
    tap_grad = taps_sum[:, :tap_count] / jnp.sqrt(f32(token_total))
    return (query_grad, key_grad, value_grad, tap_grad, -pole_sum / f32(token_total), mode_sum / f32(token_total))


def summed_all(taps_sum, mode_sum, pole_sum):
    both = summed(jnp.stack([mode_sum, pole_sum]))
    return summed(taps_sum), both[0], both[1]


def solution(mesh):
    tokens = P(("groups", "ctx", "inner"), "chan")
    return jax.shard_map(
        on_device,
        mesh=mesh,
        in_specs=(tokens, tokens, tokens, tokens, P(None, None, "chan"), P(None, "chan"), P(None, "chan")),
        out_specs=(
            tokens,
            tokens,
            tokens,
            P("groups", None, "chan"),
            P("groups", "chan"),
            P("groups", "chan"),
        ),
        check_vma=False,
    )
```

time: 747 us -> 206 us (0.28); the launches traced: 733 us -> 205 us
  local copies, waits for them, and re-layouts: 411 us -> 3.08 us
  other arithmetic: 163 us -> 1.95 us
  Pallas kernels: 0 us -> 86.6 us
  blocking collectives: 67.7 us -> 0 us
  starting transfers between devices: 16.5 us -> 37 us
  waiting for transfers between devices: 55 us -> 75.5 us
  between operations: 15.2 us -> 0.9 us
    reshape x34 -> x0, local copies, waits for them, and re-layouts: 106 us -> none  [the longest x32 101 us: spread(): return jnp.repeat(table, members, axis=1)]
    broadcast_in_dim x33 -> x0, local copies, waits for them, and re-layouts: 92.8 us -> none  [spread(): return jnp.repeat(table, members, axis=1)]
    pallas_call x0 -> x2, Pallas kernels: none -> 86.6 us  [the longest x1 63.4 us: on_device(): pl.pallas_call(functools.partial(second_kernel, members), grid=(chans //...]
    slice x40 -> x1, local copies, waits for them, and re-layouts: 85.9 us -> 0.03 us  [on_device(): after[:3]]
    ppermute x6 -> x16, waiting for transfers between devices: 0.02 us -> 75.5 us  [the longest x10 50 us: moved(): lax.ppermute(block, LINE, [(i, i + distance) for i in devices if i + dist...]
    another operation x25 -> x2, local copies, waits for them, and re-layouts: 73 us -> 2.03 us  [on_device(): jnp.stack([x[:SUB] for x in (queries, keys_in, values_in, out_grad)])]
    reduce_sum x28 -> x0, other arithmetic: 65.4 us -> none  [the longest x16 29.3 us: retreat(): out_rows.append(jnp.sum(residue_rows * running, axis=0))]
    add x40 -> x9, other arithmetic: 58.5 us -> 0.42 us  [the longest x4 0.29 us: carried_in(): state = state + decay * moved(state, sign * distance)]
  transfers between devices with their start and end apart: 9 -> 16, of which waited for: 2 -> 11; matrix products, arithmetic and copies ran while one was open for 28% -> 0% of each run, Pallas kernels for 0% -> 0%
where the time goes in v1:
time: 206 us; the launch traced here: 205 us
  Pallas kernels  86.6 us (42%)
  waiting for transfers between devices  75.5 us (37%)
  starting transfers between devices  37 us (18%)
  local copies, waits for them, and re-layouts  3.08 us (1%)
    pallas_call x1, Pallas kernels, on_device(): pl.pallas_call(functools.partial(second_kernel, members), grid=(chans //...  63.4 us
    ppermute x10, waiting for transfers between devices, moved(): lax.ppermute(block, LINE, [(i, i + distance) for i in devices if i + dist...  50 us
    ppermute x10, starting transfers between devices, moved(): lax.ppermute(block, LINE, [(i, i + distance) for i in devices if i + dist...  26.5 us
    ppermute x6, waiting for transfers between devices, summed(): lax.ppermute(block, LINE, [(i, i ^ distance) for i in range(count)])  25.5 us
    pallas_call x1, Pallas kernels, on_device(): pl.pallas_call(functools.partial(first_kernel, members), grid=(chans // w...  23.2 us
    ppermute x6, starting transfers between devices, summed(): lax.ppermute(block, LINE, [(i, i ^ distance) for i in range(count)])  10.6 us
  transfers between devices with their start and end apart: 16, of which 11 were waited for; matrix products, arithmetic and copies ran while one was open for 0% of the time, Pallas kernels for 0%

profile of v1, /device:TPU:0, one launch (start us, length us, event | category | flops | bytes accessed | tf_op | source)
XLA Modules:
  0.0 205.1 jit_solution(11777170666404278124)
XLA Ops:
  0.6 0.0 copy-start
  0.6 0.0 copy-start.2
  0.7 0.0 copy-start.1
  0.7 0.0 copy-start.5
  0.7 0.0 copy-start.4
  0.7 1.1 slice_bitcast_fusion.4
  1.8 1.0 slice_bitcast_fusion.2
  2.8 1.3 collective-permute-start.1
  4.1 5.5 %collective-permute-start = (bf16[3,8,4096]{2,1,0:T(8,128)(2,1)S(1)}, bf16[3,8,4096]{2,1,0:T(8,128)(2,1)S(1)}, u32[]{:S(2)}, u32[]{:S(2)}) collective-permute-start(bf16[3,8,4096]{2,1,0:T(8,128)(2,1)S(1)} %pad_maximum_fusion.1), channel_id=1, source_target_pairs={{0,2},{2,4},{4,6},{6,8},{8,10},{10,12},{12,14},{1,3},{3,5},{5,7},{... | collective-permute-start | bytes 589832 | tf_op jit(solution)/shard_map/ppermute | solution.py:18
  9.6 8.7 %collective-permute-done = bf16[3,8,4096]{2,1,0:T(8,128)(2,1)S(1)} collective-permute-done((bf16[3,8,4096]{2,1,0:T(8,128)(2,1)S(1)}, bf16[3,8,4096]{2,1,0:T(8,128)(2,1)S(1)}, u32[]{:S(2)}, u32[]{:S(2)}) %collective-permute-start) | collective-permute-done | bytes 196640 | tf_op jit(solution)/shard_map/ppermute | solution.py:18
  18.3 0.0 collective-permute-done.1
  18.3 0.0 copy-done
  18.4 0.0 copy-done.2
  18.4 0.0 copy-done.1
  18.4 0.0 copy-done.5
  18.4 0.0 copy-done.4
  18.4 0.0 copy-start.3
  18.4 1.0 copy-done.3
  19.4 23.2 %local_states.1 = (f32[3,136,4096]{2,1,0:T(8,128)}, f32[16,8,4096]{2,1,0:T(8,128)}, f32[16,8,4096]{2,1,0:T(8,128)}, f32[16,4096]{1,0:T(8,128)S(1)}, f32[16,4096]...) custom-call(bf16[128,4096]{1,0:T(8,128)(2,1)S(1)} %copy-done, bf16[128,4096]{1,0:T(8,128)(2,1)S(1)} %copy-done.1, ...), custom_call_target="tpu_custom_call" | custom-call | tf_op jit(solution)/shard_map/local_states/pallas_call | solution.py:241
  42.6 1.3 collective-permute-start.6
  43.9 5.0 %collective-permute-start.2 = (f32[16,4096]{1,0:T(8,128)S(1)}, f32[16,4096]{1,0:T(8,128)S(1)}, u32[]{:S(2)}, u32[]{:S(2)}) collective-permute-start(f32[16,4096]{1,0:T(8,128)S(1)} %get-tuple-element.22.final_ref), channel_id=1, source_target_pairs={{0,2},{2,4},{4,6},{6,8},{8,10},{10,12},{12,14},{1,3},{3,5},{5,7},{... | collective-permute-start | bytes 786440 | tf_op jit(solution)/shard_map/ppermute | solution.py:18
  49.0 4.5 %collective-permute-done.6 = f32[16,4096]{1,0:T(8,128)S(1)} collective-permute-done((f32[16,4096]{1,0:T(8,128)S(1)}, f32[16,4096]{1,0:T(8,128)S(1)}, u32[]{:S(2)}, u32[]{:S(2)}) %collective-permute-start.6) | collective-permute-done | bytes 262176 | tf_op jit(solution)/shard_map/ppermute | solution.py:18
  53.5 1.3 collective-permute-start.7
  54.8 4.5 %collective-permute-done.2 = f32[16,4096]{1,0:T(8,128)S(1)} collective-permute-done((f32[16,4096]{1,0:T(8,128)S(1)}, f32[16,4096]{1,0:T(8,128)S(1)}, u32[]{:S(2)}, u32[]{:S(2)}) %collective-permute-start.2) | collective-permute-done | bytes 262176 | tf_op jit(solution)/shard_map/ppermute | solution.py:18
  59.3 4.4 %collective-permute-start.3 = (f32[16,4096]{1,0:T(8,128)S(1)}, f32[16,4096]{1,0:T(8,128)S(1)}, u32[]{:S(2)}, u32[]{:S(2)}) collective-permute-start(f32[16,4096]{1,0:T(8,128)S(1)} %collective-permute-done.2), channel_id=1, source_target_pairs={{0,2},{2,4},{4,6},{6,8},{8,10},{10,12},{12,14},{1,3},{3,5},{5,7},{... | collective-permute-start | bytes 786440 | tf_op jit(solution)/shard_map/ppermute | solution.py:18
  63.7 0.0 collective-permute-done.7
  63.7 0.1 multiply_add_fusion.2
  63.8 1.3 collective-permute-start.8
  65.1 8.1 %collective-permute-done.3 = f32[16,4096]{1,0:T(8,128)S(1)} collective-permute-done((f32[16,4096]{1,0:T(8,128)S(1)}, f32[16,4096]{1,0:T(8,128)S(1)}, u32[]{:S(2)}, u32[]{:S(2)}) %collective-permute-start.3) | collective-permute-done | bytes 262176 | tf_op jit(solution)/shard_map/ppermute | solution.py:18
  73.1 9.7 %collective-permute-done.8 = f32[16,4096]{1,0:T(8,128)S(1)} collective-permute-done((f32[16,4096]{1,0:T(8,128)S(1)}, f32[16,4096]{1,0:T(8,128)S(1)}, u32[]{:S(2)}, u32[]{:S(2)}) %collective-permute-start.8) | collective-permute-done | bytes 262176 | tf_op jit(solution)/shard_map/ppermute | solution.py:18
  82.9 0.1 multiply_add_fusion.1
  83.0 1.3 collective-permute-start.9
  84.3 3.7 %collective-permute-start.4 = (f32[16,4096]{1,0:T(8,128)S(1)}, f32[16,4096]{1,0:T(8,128)S(1)}, u32[]{:S(2)}, u32[]{:S(2)}) collective-permute-start(f32[16,4096]{1,0:T(8,128)S(1)} %get-tuple-element.41), channel_id=1, source_target_pairs={{0,4},{2,6},{4,8},{6,10},{8,12},{10,14},{1,5},{3,7},{5,9},{7,11},{... | collective-permute-start | bytes 786440 | tf_op jit(solution)/shard_map/ppermute | solution.py:18
  88.0 9.5 %collective-permute-done.9 = f32[16,4096]{1,0:T(8,128)S(1)} collective-permute-done((f32[16,4096]{1,0:T(8,128)S(1)}, f32[16,4096]{1,0:T(8,128)S(1)}, u32[]{:S(2)}, u32[]{:S(2)}) %collective-permute-start.9) | collective-permute-done | bytes 262176 | tf_op jit(solution)/shard_map/ppermute | solution.py:18
  97.5 0.0 collective-permute-done.4
  97.5 0.1 multiply_add_fusion
  97.6 1.5 collective-permute-start.5
  99.1 4.9 %collective-permute-done.5 = f32[16,4096]{1,0:T(8,128)S(1)} collective-permute-done((f32[16,4096]{1,0:T(8,128)S(1)}, f32[16,4096]{1,0:T(8,128)S(1)}, u32[]{:S(2)}, u32[]{:S(2)}) %collective-permute-start.5) | collective-permute-done | bytes 262176 | tf_op jit(solution)/shard_map/ppermute | solution.py:18
  104.0 0.1 multiply_add_fusion.3.sin_ref
  104.1 63.4 %gradients.1 = (bf16[128,4096]{1,0:T(8,128)(2,1)}, bf16[128,4096]{1,0:T(8,128)(2,1)}, bf16[128,4096]{1,0:T(8,128)(2,1)}, f32[3,8,4096]{2,1,0:T(8,128)S(1)}, f32[...) custom-call(bf16[128,4096]{1,0:T(8,128)(2,1)S(1)} %copy-done, bf16[128,4096]{1,0:T(8,128)(2,1)S(1)} %copy-done.1, ...), custom_call_target="tpu_custom_call" | custom-call | tf_op jit(solution)/shard_map/gradients/pallas_call | solution.py:262
  167.5 0.1 collective-permute-start.10
  167.5 9.3 %collective-permute-done.10 = f32[3,8,4096]{2,1,0:T(8,128)S(1)} collective-permute-done((f32[3,8,4096]{2,1,0:T(8,128)S(1)}, f32[3,8,4096]{2,1,0:T(8,128)S(1)}, u32[]{:S(2)}, u32[]{:S(2)}) %collective-permute-start.10) | collective-permute-done | bytes 393248 | tf_op jit(solution)/shard_map/ppermute | solution.py:37
  176.8 0.1 add.42
  176.9 3.1 %collective-permute-start.11 = (f32[3,8,4096]{2,1,0:T(8,128)S(1)}, f32[3,8,4096]{2,1,0:T(8,128)S(1)}, u32[]{:S(2)}, u32[]{:S(2)}) collective-permute-start(f32[3,8,4096]{2,1,0:T(8,128)S(1)} %add.42), channel_id=1, source_target_pairs={{0,4},{2,6},{4,0},{6,2},{8,12},{10,14},{12,8},{14,10},{1,5},{3,7},... | collective-permute-start | bytes 1179656 | tf_op jit(solution)/shard_map/ppermute | solution.py:37
  180.0 0.0 collective-permute-start.13
  180.0 3.9 %collective-permute-done.13 = f32[2,16,256]{2,1,0:T(8,128)S(1)} collective-permute-done((f32[2,16,256]{2,1,0:T(8,128)S(1)}, f32[2,16,256]{2,1,0:T(8,128)S(1)}, u32[]{:S(2)}, u32[]{:S(2)}) %collective-permute-start.13) | collective-permute-done | bytes 32800 | tf_op jit(solution)/shard_map/ppermute | solution.py:37
  183.9 0.1 collective-permute-start.14
  184.0 2.3 %collective-permute-done.11 = f32[3,8,4096]{2,1,0:T(8,128)S(1)} collective-permute-done((f32[3,8,4096]{2,1,0:T(8,128)S(1)}, f32[3,8,4096]{2,1,0:T(8,128)S(1)}, u32[]{:S(2)}, u32[]{:S(2)}) %collective-permute-start.11) | collective-permute-done | bytes 393248 | tf_op jit(solution)/shard_map/ppermute | solution.py:37
  186.3 0.1 add.43
  186.4 6.6 %collective-permute-start.12 = (f32[3,8,4096]{2,1,0:T(8,128)S(1)}, f32[3,8,4096]{2,1,0:T(8,128)S(1)}, u32[]{:S(2)}, u32[]{:S(2)}) collective-permute-start(f32[3,8,4096]{2,1,0:T(8,128)S(1)} %add.43), channel_id=1, source_target_pairs={{0,8},{2,10},{4,12},{6,14},{8,0},{10,2},{12,4},{14,6},{1,9},{3,11}... | collective-permute-start | bytes 1179656 | tf_op jit(solution)/shard_map/ppermute | solution.py:37
  193.0 0.0 collective-permute-done.14
  193.0 0.6 collective-permute-start.15
  193.7 10.0 %collective-permute-done.15 = f32[2,16,256]{2,1,0:T(8,128)S(1)} collective-permute-done((f32[2,16,256]{2,1,0:T(8,128)S(1)}, f32[2,16,256]{2,1,0:T(8,128)S(1)}, u32[]{:S(2)}, u32[]{:S(2)}) %collective-permute-start.15) | collective-permute-done | bytes 32800 | tf_op jit(solution)/shard_map/ppermute | solution.py:37
  203.7 0.6 fusion.1
  204.3 0.0 collective-permute-done.12
  204.3 0.8 fusion
  (10 shorter events, 0.2 us)
Async XLA Ops:
  0.6 17.7 %copy-start = (bf16[128,4096]{1,0:T(8,128)(2,1)S(1)}, bf16[128,4096]{1,0:T(8,128)(2,1)}, u32[]{:S(2)}) copy-start(bf16[128,4096]{1,0:T(8,128)(2,1)} %q_ref.3) | copy-start | bytes 3145732
  0.6 17.7 %copy-start.2 = (bf16[128,4096]{1,0:T(8,128)(2,1)S(1)}, bf16[128,4096]{1,0:T(8,128)(2,1)}, u32[]{:S(2)}) copy-start(bf16[128,4096]{1,0:T(8,128)(2,1)} %v_ref.3) | copy-start | bytes 3145732
  0.7 17.7 %copy-start.1 = (bf16[128,4096]{1,0:T(8,128)(2,1)S(1)}, bf16[128,4096]{1,0:T(8,128)(2,1)}, u32[]{:S(2)}) copy-start(bf16[128,4096]{1,0:T(8,128)(2,1)} %k_ref.3) | copy-start | bytes 3145732
  0.7 17.7 %copy-start.5 = (f32[16,256]{1,0:T(8,128)S(1)}, f32[16,256]{1,0:T(8,128)}, u32[]{:S(2)}) copy-start(f32[16,256]{1,0:T(8,128)} %res_ref.1) | copy-start | bytes 49156
  0.7 17.7 %copy-start.4 = (f32[16,256]{1,0:T(8,128)S(1)}, f32[16,256]{1,0:T(8,128)}, u32[]{:S(2)}) copy-start(f32[16,256]{1,0:T(8,128)} %rate_ref.1) | copy-start | bytes 49156
  2.8 15.5 %collective-permute-start.1 = (bf16[4,8,4096]{2,1,0:T(8,128)(2,1)S(1)}, bf16[4,8,4096]{2,1,0:T(8,128)(2,1)S(1)}, u32[]{:S(2)}, u32[]{:S(2)}) collective-permute-start(bf16[4,8,4096]{2,1,0:T(8,128)(2,1)S(1)} %pad_maximum_fusion), channel_id=1, source_target_pairs={{2,0},{4,2},{6,4},{8,6},{10,8},{12,10},{14,12},{3,1},{5,3},{7,5},{... | collective-permute-start | bytes 786440 | tf_op jit(solution)/shard_map/ppermute | solution.py:18
  4.1 14.2 %collective-permute-start = (bf16[3,8,4096]{2,1,0:T(8,128)(2,1)S(1)}, bf16[3,8,4096]{2,1,0:T(8,128)(2,1)S(1)}, u32[]{:S(2)}, u32[]{:S(2)}) collective-permute-start(bf16[3,8,4096]{2,1,0:T(8,128)(2,1)S(1)} %pad_maximum_fusion.1), channel_id=1, source_target_pairs={{0,2},{2,4},{4,6},{6,8},{8,10},{10,12},{12,14},{1,3},{3,5},{5,7},{... | collective-permute-start | bytes 589832 | tf_op jit(solution)/shard_map/ppermute | solution.py:18
  18.4 1.0 copy-start.3
  42.6 10.9 %collective-permute-start.6 = (f32[16,4096]{1,0:T(8,128)S(1)}, f32[16,4096]{1,0:T(8,128)S(1)}, u32[]{:S(2)}, u32[]{:S(2)}) collective-permute-start(f32[16,4096]{1,0:T(8,128)S(1)} %get-tuple-element.25), channel_id=1, source_target_pairs={{2,0},{4,2},{6,4},{8,6},{10,8},{12,10},{14,12},{3,1},{5,3},{7,5},{... | collective-permute-start | bytes 786440 | tf_op jit(solution)/shard_map/ppermute | solution.py:18
  43.9 15.3 %collective-permute-start.2 = (f32[16,4096]{1,0:T(8,128)S(1)}, f32[16,4096]{1,0:T(8,128)S(1)}, u32[]{:S(2)}, u32[]{:S(2)}) collective-permute-start(f32[16,4096]{1,0:T(8,128)S(1)} %get-tuple-element.22.final_ref), channel_id=1, source_target_pairs={{0,2},{2,4},{4,6},{6,8},{8,10},{10,12},{12,14},{1,3},{3,5},{5,7},{... | collective-permute-start | bytes 786440 | tf_op jit(solution)/shard_map/ppermute | solution.py:18
  53.5 10.2 %collective-permute-start.7 = (f32[16,4096]{1,0:T(8,128)S(1)}, f32[16,4096]{1,0:T(8,128)S(1)}, u32[]{:S(2)}, u32[]{:S(2)}) collective-permute-start(f32[16,4096]{1,0:T(8,128)S(1)} %collective-permute-done.6), channel_id=1, source_target_pairs={{2,0},{4,2},{6,4},{8,6},{10,8},{12,10},{14,12},{3,1},{5,3},{7,5},{... | collective-permute-start | bytes 786440 | tf_op jit(solution)/shard_map/ppermute | solution.py:18
  59.3 13.9 %collective-permute-start.3 = (f32[16,4096]{1,0:T(8,128)S(1)}, f32[16,4096]{1,0:T(8,128)S(1)}, u32[]{:S(2)}, u32[]{:S(2)}) collective-permute-start(f32[16,4096]{1,0:T(8,128)S(1)} %collective-permute-done.2), channel_id=1, source_target_pairs={{0,2},{2,4},{4,6},{6,8},{8,10},{10,12},{12,14},{1,3},{3,5},{5,7},{... | collective-permute-start | bytes 786440 | tf_op jit(solution)/shard_map/ppermute | solution.py:18
  63.8 19.1 %collective-permute-start.8 = (f32[16,4096]{1,0:T(8,128)S(1)}, f32[16,4096]{1,0:T(8,128)S(1)}, u32[]{:S(2)}, u32[]{:S(2)}) collective-permute-start(f32[16,4096]{1,0:T(8,128)S(1)} %multiply_add_fusion.2), channel_id=1, source_target_pairs={{4,0},{6,2},{8,4},{10,6},{12,8},{14,10},{5,1},{7,3},{9,5},{11,7},{... | collective-permute-start | bytes 786440 | tf_op jit(solution)/shard_map/ppermute | solution.py:18
  83.0 14.5 %collective-permute-start.9 = (f32[16,4096]{1,0:T(8,128)S(1)}, f32[16,4096]{1,0:T(8,128)S(1)}, u32[]{:S(2)}, u32[]{:S(2)}) collective-permute-start(f32[16,4096]{1,0:T(8,128)S(1)} %get-tuple-element.40), channel_id=1, source_target_pairs={{8,0},{10,2},{12,4},{14,6},{9,1},{11,3},{13,5},{15,7},{24,16},{26,... | collective-permute-start | bytes 786440 | tf_op jit(solution)/shard_map/ppermute | solution.py:18
  84.3 13.3 %collective-permute-start.4 = (f32[16,4096]{1,0:T(8,128)S(1)}, f32[16,4096]{1,0:T(8,128)S(1)}, u32[]{:S(2)}, u32[]{:S(2)}) collective-permute-start(f32[16,4096]{1,0:T(8,128)S(1)} %get-tuple-element.41), channel_id=1, source_target_pairs={{0,4},{2,6},{4,8},{6,10},{8,12},{10,14},{1,5},{3,7},{5,9},{7,11},{... | collective-permute-start | bytes 786440 | tf_op jit(solution)/shard_map/ppermute | solution.py:18
  97.6 6.4 %collective-permute-start.5 = (f32[16,4096]{1,0:T(8,128)S(1)}, f32[16,4096]{1,0:T(8,128)S(1)}, u32[]{:S(2)}, u32[]{:S(2)}) collective-permute-start(f32[16,4096]{1,0:T(8,128)S(1)} %get-tuple-element.39), channel_id=1, source_target_pairs={{0,8},{2,10},{4,12},{6,14},{1,9},{3,11},{5,13},{7,15},{16,24},{18,... | collective-permute-start | bytes 786440 | tf_op jit(solution)/shard_map/ppermute | solution.py:18
  167.5 9.3 %collective-permute-start.10 = (f32[3,8,4096]{2,1,0:T(8,128)S(1)}, f32[3,8,4096]{2,1,0:T(8,128)S(1)}, u32[]{:S(2)}, u32[]{:S(2)}) collective-permute-start(f32[3,8,4096]{2,1,0:T(8,128)S(1)} %get-tuple-element.29), channel_id=1, source_target_pairs={{0,2},{2,0},{4,6},{6,4},{8,10},{10,8},{12,14},{14,12},{1,3},{3,1},... | collective-permute-start | bytes 1179656 | tf_op jit(solution)/shard_map/ppermute | solution.py:37
  176.9 9.5 %collective-permute-start.11 = (f32[3,8,4096]{2,1,0:T(8,128)S(1)}, f32[3,8,4096]{2,1,0:T(8,128)S(1)}, u32[]{:S(2)}, u32[]{:S(2)}) collective-permute-start(f32[3,8,4096]{2,1,0:T(8,128)S(1)} %add.42), channel_id=1, source_target_pairs={{0,4},{2,6},{4,0},{6,2},{8,12},{10,14},{12,8},{14,10},{1,5},{3,7},... | collective-permute-start | bytes 1179656 | tf_op jit(solution)/shard_map/ppermute | solution.py:37
  180.0 3.9 %collective-permute-start.13 = (f32[2,16,256]{2,1,0:T(8,128)S(1)}, f32[2,16,256]{2,1,0:T(8,128)S(1)}, u32[]{:S(2)}, u32[]{:S(2)}) collective-permute-start(f32[2,16,256]{2,1,0:T(8,128)S(1)} %pad_maximum_fusion.2), channel_id=1, source_target_pairs={{0,2},{2,0},{4,6},{6,4},{8,10},{10,8},{12,14},{14,12},{1,3},{3,1},... | collective-permute-start | bytes 98312 | tf_op jit(solution)/shard_map/ppermute | solution.py:37
  183.9 9.1 %collective-permute-start.14 = (f32[2,16,256]{2,1,0:T(8,128)S(1)}, f32[2,16,256]{2,1,0:T(8,128)S(1)}, u32[]{:S(2)}, u32[]{:S(2)}) collective-permute-start(f32[2,16,256]{2,1,0:T(8,128)S(1)} %fusion.4), channel_id=1, source_target_pairs={{0,4},{2,6},{4,0},{6,2},{8,12},{10,14},{12,8},{14,10},{1,5},{3,7},... | collective-permute-start | bytes 98312 | tf_op jit(solution)/shard_map/ppermute | solution.py:37
  186.4 17.9 %collective-permute-start.12 = (f32[3,8,4096]{2,1,0:T(8,128)S(1)}, f32[3,8,4096]{2,1,0:T(8,128)S(1)}, u32[]{:S(2)}, u32[]{:S(2)}) collective-permute-start(f32[3,8,4096]{2,1,0:T(8,128)S(1)} %add.43), channel_id=1, source_target_pairs={{0,8},{2,10},{4,12},{6,14},{8,0},{10,2},{12,4},{14,6},{1,9},{3,11}... | collective-permute-start | bytes 1179656 | tf_op jit(solution)/shard_map/ppermute | solution.py:37
  193.0 10.7 %collective-permute-start.15 = (f32[2,16,256]{2,1,0:T(8,128)S(1)}, f32[2,16,256]{2,1,0:T(8,128)S(1)}, u32[]{:S(2)}, u32[]{:S(2)}) collective-permute-start(f32[2,16,256]{2,1,0:T(8,128)S(1)} %fusion.5), channel_id=1, source_target_pairs={{0,8},{2,10},{4,12},{6,14},{8,0},{10,2},{12,4},{14,6},{1,9},{3,11}... | collective-permute-start | bytes 98312 | tf_op jit(solution)/shard_map/ppermute | solution.py:37

commit v2 on v1

--- a/solution.py
+++ b/solution.py
@@ -10,6 +10,9 @@
 LINE = ("ctx", "inner")
 LANES = 128
 SUB = 8
+TOGETHER = 4
+PIECE = 1024
+MESH = pl.DeviceIdType.MESH
 EXACT = lax.Precision.HIGHEST
 
 
@@ -18,25 +21,236 @@
     return lax.ppermute(block, LINE, [(i, i + distance) for i in devices if i + distance in devices])
 
 
-def carried_in(total, decay, reverse):
-    sign = -1 if reverse else 1
+def place_of(position):
+    inner = lax.axis_size("inner")
+    return {"ctx": position // inner, "inner": position % inner}
+
+
+def carry_kernel(pieces, rows, final_ref, first_ref, rates_ref, sin_ref, pin_ref, near, outward, entering,
+                 near_send, near_recv, far_send, far_recv, give_send, give_recv):
+    inner, outer = lax.axis_size("inner"), lax.axis_size("ctx")
+    x, z = lax.axis_index("inner"), lax.axis_index("ctx")
+    width = final_ref.shape[1] // pieces
+    barrier = pltpu.get_barrier_semaphore()
+    others = [lax.rem(x + d, inner) for d in range(1, inner)]
+    for other in others:
+        pl.semaphore_signal(barrier, inc=1, device_id={"inner": other}, device_id_type=MESH)
+
+    @pl.when(z > 0)
+    def _():
+        pl.semaphore_signal(barrier, inc=1, device_id={"ctx": z - 1}, device_id_type=MESH)
+
+    @pl.when(z < outer - 1)
+    def _():
+        pl.semaphore_signal(barrier, inc=1, device_id={"ctx": z + 1}, device_id_type=MESH)
+
+    pl.semaphore_wait(barrier, inner - 1 + jnp.where(z > 0, 1, 0) + jnp.where(z < outer - 1, 1, 0))
+
+    def copy(source, target, send, recv, where):
+        return pltpu.make_async_remote_copy(
+            src_ref=source, dst_ref=target, send_sem=send, recv_sem=recv, device_id=where, device_id_type=MESH
+        )
+
+    lines = []
+    for line, total_ref, into_ref in ((0, final_ref, sin_ref), (1, first_ref, pin_ref)):
+        xs, zs = (x, z) if line == 0 else (inner - 1 - x, outer - 1 - z)
+        lines.append((line, total_ref, into_ref, xs, zs, 1 if line == 0 else -1))
+
+    def near_copy(line, total_ref, piece, steps, sign):
+        cols = pl.ds(piece * width, width)
+        return copy(
+            total_ref.at[:, cols], near.at[line, steps - 1, :, cols],
+            near_send.at[line, steps - 1, piece], near_recv.at[line, steps - 1, piece],
+            {"inner": lax.rem(x + sign * steps + inner, inner)},
+        )
+
+    def far_copy(line, piece, sign):
+        cols = pl.ds(piece * width, width)
+        return copy(
+            outward.at[line, :, cols], entering.at[line, :, cols],
+            far_send.at[line, piece], far_recv.at[line, piece],
+            {"ctx": lax.rem(z + sign + outer, outer)},
+        )
+
+    def give_copy(line, piece, steps, sign):
+        cols = pl.ds(piece * width, width)
+        return copy(
+            entering.at[line, :, cols], entering.at[line, :, cols],
+            give_send.at[line, steps - 1, piece], give_recv.at[line, piece],
+            {"inner": lax.rem(x - sign * steps + inner, inner)},
+        )
+
+    for piece in range(pieces):
+        for line, total_ref, _, xs, _, sign in lines:
+            for steps in range(1, inner):
+                @pl.when(xs + steps < inner)
+                def _():
+                    near_copy(line, total_ref, piece, steps, sign).start()
+
+    for piece in range(pieces):
+        cols = pl.ds(piece * width, width)
+        decay = jnp.exp(rates_ref[:, cols] * -float(rows))
+        for line, total_ref, into_ref, xs, zs, sign in lines:
+            @pl.when(xs == inner - 1)
+            def _():
+                total = jnp.zeros_like(into_ref[:, cols])
+                for steps in range(inner - 1, 0, -1):
+                    near_copy(line, total_ref, piece, steps, sign).wait_recv()
+                    total = decay * total + near[line, steps - 1, :, cols]
+                into_ref[:, cols] = total
+
+                @pl.when(zs == 0)
+                def _():
+                    entering[line, :, cols] = jnp.zeros_like(total)
+
+                @pl.when(zs > 0)
+                def _():
+                    far_copy(line, piece, sign).wait_recv()
+
+                power = jnp.exp(rates_ref[:, cols] * -float(rows * (inner - 1)))
+                mine = power * entering[line, :, cols] + into_ref[:, cols]
+                into_ref[:, cols] = mine
+
+                @pl.when(zs < outer - 1)
+                def _():
+                    outward[line, :, cols] = decay * mine + total_ref[:, cols]
+                    far_copy(line, piece, sign).start()
+
+                for steps in range(1, inner):
+                    give_copy(line, piece, steps, sign).start()
+
+    for piece in range(pieces):
+        cols = pl.ds(piece * width, width)
+        decay = jnp.exp(rates_ref[:, cols] * -float(rows))
+        for line, total_ref, into_ref, xs, zs, sign in lines:
+            @pl.when(xs < inner - 1)
+            def _():
+                into_ref[:, cols] = jnp.zeros_like(into_ref[:, cols])
+                for steps in range(inner - 2, 0, -1):
+                    @pl.when(xs >= steps)
+                    def _():
+                        near_copy(line, total_ref, piece, steps, sign).wait_recv()
+                        into_ref[:, cols] = decay * into_ref[:, cols] + near[line, steps - 1, :, cols]
+
+                give_copy(line, piece, 1, sign).wait_recv()
+                power = jnp.exp(rates_ref[:, cols] * (-float(rows) * xs.astype(jnp.float32)))
+                into_ref[:, cols] = power * entering[line, :, cols] + into_ref[:, cols]
+
+    for piece in range(pieces):
+        for line, total_ref, _, xs, zs, sign in lines:
+            for steps in range(1, inner):
+                @pl.when(xs + steps < inner)
+                def _():
+                    near_copy(line, total_ref, piece, steps, sign).wait_send()
+
+                @pl.when(xs == inner - 1)
+                def _():
+                    give_copy(line, piece, steps, sign).wait_send()
+
+            @pl.when((xs == inner - 1) & (zs < outer - 1))
+            def _():
+                far_copy(line, piece, sign).wait_send()
+
+
+def carried(final, first, rates, rows):
+    modes, chans = final.shape
+    pieces = max(1, chans // PIECE)
+    hops = max(1, lax.axis_size("inner") - 1)
+    shape = jax.ShapeDtypeStruct((modes, chans), jnp.float32)
+    vmem = pl.BlockSpec(memory_space=pltpu.VMEM)
+    return pl.pallas_call(
+        functools.partial(carry_kernel, pieces, rows),
+        in_specs=[vmem] * 3,
+        out_specs=[vmem] * 2,
+        out_shape=[shape] * 2,
+        scratch_shapes=[
+            pltpu.VMEM((2, hops, modes, chans), jnp.float32),
+            pltpu.VMEM((2, modes, chans), jnp.float32),
+            pltpu.VMEM((2, modes, chans), jnp.float32),
+            pltpu.SemaphoreType.DMA((2, hops, pieces)),
+            pltpu.SemaphoreType.DMA((2, hops, pieces)),
+            pltpu.SemaphoreType.DMA((2, pieces)),
+            pltpu.SemaphoreType.DMA((2, pieces)),
+            pltpu.SemaphoreType.DMA((2, hops, pieces)),
+            pltpu.SemaphoreType.DMA((2, pieces)),
+        ],
+        compiler_params=pltpu.CompilerParams(
+            collective_id=0, has_side_effects=True, vmem_limit_bytes=16 * 1024 * 1024
+        ),
+        name="carry",
+    )(final, first, rates)
+
+
+def sum_kernel(x_ref, out_ref, land, send_sem, recv_sem):
     count = lax.axis_size(LINE)
-    state = moved(total, sign)
-    distance = 1
-    while distance < count - 1:
-        state = state + decay * moved(state, sign * distance)
-        decay = decay * decay
-        distance *= 2
-    return state
+    me = lax.axis_index("ctx") * lax.axis_size("inner") + lax.axis_index("inner")
+    barrier = pltpu.get_barrier_semaphore()
+    others = [lax.rem(me + d, count) for d in range(1, count)]
+    for other in others:
+        pl.semaphore_signal(barrier, inc=1, device_id=place_of(other), device_id_type=MESH)
+    pl.semaphore_wait(barrier, count - 1)
+
+    def copy_of(source, target, phase, d):
+        return pltpu.make_async_remote_copy(
+            src_ref=source,
+            dst_ref=target,
+            send_sem=send_sem.at[phase, d],
+            recv_sem=recv_sem.at[phase, d],
+            device_id=place_of(others[d]),
+            device_id_type=MESH,
+        )
+
+    copies = [copy_of(x_ref.at[other], land.at[d], 0, d) for d, other in enumerate(others)]
+    for copy in copies:
+        copy.start()
+    total = x_ref[me]
+    for d, copy in enumerate(copies):
+        copy.wait_recv()
+        total = total + land[d]
+    out_ref[me] = total
+    spreads = [copy_of(out_ref.at[me], out_ref.at[me], 1, d) for d in range(count - 1)]
+    for copy in spreads:
+        copy.start()
+    for copy in copies:
+        copy.wait_send()
+    for d in range(count - 1):
+        source = lax.rem(me + count - 1 - d, count)
+        copy_of(out_ref.at[me], out_ref.at[source], 1, d).wait_recv()
+    for copy in spreads:
+        copy.wait_send()
 
 
 def summed(block):
     count = lax.axis_size(LINE)
-    distance = 1
-    while distance < count:
-        block = block + lax.ppermute(block, LINE, [(i, i ^ distance) for i in range(count)])
-        distance *= 2
-    return block
+    rows = block.shape[0]
+    each = -(-rows // (count * SUB)) * SUB
+    padded = jnp.pad(block, ((0, each * count - rows), (0, 0))).reshape(count, each, LANES)
+    vmem = pl.BlockSpec(memory_space=pltpu.VMEM)
+    result = pl.pallas_call(
+        sum_kernel,
+        in_specs=[vmem],
+        out_specs=vmem,
+        out_shape=jax.ShapeDtypeStruct(padded.shape, jnp.float32),
+        scratch_shapes=[
+            pltpu.VMEM((count - 1, each, LANES), jnp.float32),
+            pltpu.SemaphoreType.DMA((2, count - 1)),
+            pltpu.SemaphoreType.DMA((2, count - 1)),
+        ],
+        compiler_params=pltpu.CompilerParams(
+            collective_id=1, has_side_effects=True, vmem_limit_bytes=16 * 1024 * 1024
+        ),
+        name="sums",
+    )(padded)
+    return result.reshape(count * each, LANES)[:rows]
+
+
+def tiles(block):
+    lead, sub, chans = block.shape
+    return block.reshape(lead, sub, chans // LANES, LANES).transpose(0, 2, 1, 3).reshape(-1, LANES)
+
+
+def untiled(flat, lead, sub, chans):
+    return flat.reshape(lead, chans // LANES, sub, LANES).transpose(0, 2, 1, 3).reshape(lead, sub, chans)
 
 
 def spread_matrix(local_groups, width, members):
@@ -104,7 +318,7 @@
 def second_kernel(members, q_ref, k_ref, v_ref, g_ref, prev_ref, gnext_ref, taps_ref, mix_ref, ef_ref, ea_ref,
                   final_ref, rates_ref, ress_ref, sin_ref, pin_ref,
                   qg_ref, kg_ref, vg_ref, tap_ref, mode_ref, pole_ref,
-                  wide, src, adj, long_out, long_adj, back, mode_rows, pole_rows, each):
+                  wide, src, adj, long_out, long_adj, back, mode_rows, pole_rows, each, sums, terms, held):
     rows, width = q_ref.shape
     modes = rates_ref.shape[0]
     local_groups = mode_ref.shape[1]
@@ -127,44 +341,62 @@
 
         lam_table = jnp.exp(-rates_ref[:, cols])
         decay_table = jnp.exp(rates_ref[:, cols] * -float(steps))
-        tables = (lam_table, ress_ref[:, cols], decay_table, sin_ref[:, cols], pin_ref[:, cols])
-        for i, table in enumerate(tables):
+        for i, table in enumerate((lam_table, ress_ref[:, cols])):
             for n in range(modes):
                 each[i, n] = jnp.broadcast_to(table[n:n + 1], (SUB, LANES))
-
-        def one(n, sums):
-            outs, adjs = list(sums[0]), list(sums[1])
-            lam, res, decay = each[0, n], each[1, n], each[2, n]
-            state = jnp.where(chunk == 0, each[3, n], pltpu.roll(ef_ref[n, :, cols], 1, 0))
-            late = jnp.where(chunk == SUB - 1, each[4, n], pltpu.roll(ea_ref[n, :, cols], SUB - 1, 0))
+        for n in range(modes):
+            decay = jnp.broadcast_to(decay_table[n:n + 1], (SUB, LANES))
+            state = jnp.where(chunk == 0, sin_ref[n:n + 1, cols], pltpu.roll(ef_ref[n, :, cols], 1, 0))
+            late = jnp.where(
+                chunk == SUB - 1, pin_ref[n:n + 1, cols], pltpu.roll(ea_ref[n, :, cols], SUB - 1, 0)
+            )
             distance = 1
             while distance < SUB:
                 state = state + jnp.where(chunk >= distance, decay * pltpu.roll(state, distance, 0), 0.0)
                 late = late + jnp.where(chunk < SUB - distance, decay * pltpu.roll(late, SUB - distance, 0), 0.0)
                 decay = decay * decay
                 distance *= 2
-            states = [state]
-            mode_sum = zero
+            each[2, n] = state
+            each[3, n] = late
+        for j in range(steps):
+            sums[0, j] = zero
+            sums[1, j] = zero
+            terms[0, j] = s[j]
+            terms[1, j] = a[j]
+
+        @pl.loop(0, modes // TOGETHER)
+        def _(group):
+            here = [group * TOGETHER + m for m in range(TOGETHER)]
+            lam = [each[0, n] for n in here]
+            res = [each[1, n] for n in here]
+            state = [each[2, n] for n in here]
+            late = [each[3, n] for n in here]
+            mode_sum = [zero] * TOGETHER
+            pole_sum = [zero] * TOGETHER
             for j in range(steps):
-                state = lam * state + s[j]
-                states.append(state)
-                outs[j] = outs[j] + res * state
-                mode_sum = mode_sum + a[j] * state
-            pole_sum = zero
+                source, toward, out = terms[0, j], terms[1, j], sums[0, j]
+                for m in range(TOGETHER):
+                    held[m, j] = state[m]
+                    state[m] = lam[m] * state[m] + source
+                    out = out + res[m] * state[m]
+                    mode_sum[m] = mode_sum[m] + toward * state[m]
+                sums[0, j] = out
             for j in range(steps - 1, -1, -1):
-                late = lam * late + a[j]
-                adjs[j] = adjs[j] + res * late
-                pole_sum = pole_sum + late * states[j]
-            each[5, n] = mode_sum
-            each[6, n] = lam * res * pole_sum
-            return tuple(outs), tuple(adjs)
-
-        outs, adjs = lax.fori_loop(0, modes, one, ((zero,) * steps, (zero,) * steps))
-        mode_rows[:, cols] = jnp.sum(each[5], axis=1)
-        pole_rows[:, cols] = jnp.sum(each[6], axis=1)
+                toward, out = terms[1, j], sums[1, j]
+                for m in range(TOGETHER):
+                    late[m] = lam[m] * late[m] + toward
+                    out = out + res[m] * late[m]
+                    pole_sum[m] = pole_sum[m] + late[m] * held[m, j]
+                sums[1, j] = out
+            for m, n in enumerate(here):
+                each[4, n] = mode_sum[m]
+                each[5, n] = lam[m] * res[m] * pole_sum[m]
+
+        mode_rows[:, cols] = jnp.sum(each[4], axis=1)
+        pole_rows[:, cols] = jnp.sum(each[5], axis=1)
         for j in range(steps):
-            long_out[pl.ds(j, SUB, stride=steps), :] = outs[j]
-            long_adj[pl.ds(j, SUB, stride=steps), :] = adjs[j]
+            long_out[pl.ds(j, SUB, stride=steps), :] = sums[0, j]
+            long_adj[pl.ds(j, SUB, stride=steps), :] = sums[1, j]
         rate = rates_ref[:, cols]
         res = ress_ref[:, cols]
         lam = jnp.exp(-rate)
@@ -256,9 +488,7 @@
         compiler_params=params,
         name="local_states",
     )(queries, keys_in, values_in, out_grad, before, after[:3], short_taps, pole_rate, residue)
-    decay = jnp.exp(rates * -float(rows))
-    state_in = carried_in(final, decay, False)
-    late_in = carried_in(first, decay, True)
+    state_in, late_in = carried(final, first, rates, rows)
     query_grad, key_grad, value_grad, taps_sum, mode_sum, pole_sum = pl.pallas_call(
         functools.partial(second_kernel, members),
         grid=(chans // width,),
@@ -272,7 +502,9 @@
         + [pltpu.VMEM((wide_rows, LANES), f32)] * 4
         + [pltpu.VMEM((3, wide_rows, width), f32)]
         + [pltpu.VMEM((modes, width), f32)] * 2
-        + [pltpu.VMEM((7, modes, SUB, LANES), f32)],
+        + [pltpu.VMEM((6, modes, SUB, LANES), f32)]
+        + [pltpu.VMEM((2, rows // SUB, SUB, LANES), f32)] * 2
+        + [pltpu.VMEM((TOGETHER, rows // SUB, SUB, LANES), f32)],
         compiler_params=params,
         name="gradients",
     )(queries, keys_in, values_in, out_grad, before, after[3], short_taps, mix, ef, ea,
@@ -283,8 +515,15 @@
 
 
 def summed_all(taps_sum, mode_sum, pole_sum):
-    both = summed(jnp.stack([mode_sum, pole_sum]))
-    return summed(taps_sum), both[0], both[1]
+    modes, groups = mode_sum.shape
+    blocks = [taps_sum] + [x.reshape(modes // SUB, SUB, groups) for x in (mode_sum, pole_sum)]
+    parts = [tiles(x) for x in blocks]
+    total = summed(jnp.concatenate(parts, axis=0))
+    results, start = [], 0
+    for part, block in zip(parts, blocks):
+        results.append(untiled(total[start:start + part.shape[0]], *block.shape))
+        start += part.shape[0]
+    return results[0], results[1].reshape(modes, groups), results[2].reshape(modes, groups)
 
 
 def solution(mesh):

time: 206 us -> 134 us (0.65)
  waiting for transfers between devices: 75.5 us -> 8.69 us
  starting transfers between devices: 37 us -> 6.77 us
  Pallas kernels: 86.6 us -> 113 us
    pallas_call x0 -> x2, Pallas kernels: none -> 44.3 us  [the longest x1 23.7 us: carried(): pl.pallas_call(functools.partial(carry_kernel, pieces, rows), in_specs=[v...]
    ppermute x10 -> x2, waiting for transfers between devices: 50 us -> 8.69 us  [moved(): lax.ppermute(block, LINE, [(i, i + distance) for i in devices if i + dist...]
    ppermute x6 -> x0, waiting for transfers between devices: 25.5 us -> none  [summed(): lax.ppermute(block, LINE, [(i, i ^ distance) for i in range(count)])]
    ppermute x10 -> x2, starting transfers between devices: 26.5 us -> 6.77 us  [moved(): lax.ppermute(block, LINE, [(i, i + distance) for i in devices if i + dist...]
    pallas_call x1, Pallas kernels: 63.4 us -> 45.8 us  [on_device(): pl.pallas_call(functools.partial(second_kernel, members), grid=(chans //...]
    ppermute x6 -> x0, starting transfers between devices: 10.6 us -> none  [summed(): lax.ppermute(block, LINE, [(i, i ^ distance) for i in range(count)])]
  transfers between devices with their start and end apart: 16 -> 2, of which waited for: 11 -> 1; matrix products, arithmetic and copies ran while one was open for 0% -> 0% of each run, Pallas kernels for 0% -> 0%
where the time goes in v2:
time: 134 us; the launch traced here: 133 us
  Pallas kernels  113 us (84%)
  waiting for transfers between devices  8.69 us (6%)
  starting transfers between devices  6.77 us (5%)
  local copies, waits for them, and re-layouts  2.17 us (2%)
  other arithmetic  1.55 us (1%)
    pallas_call x1, Pallas kernels, on_device(): pl.pallas_call(functools.partial(second_kernel, members), grid=(chans //...  45.8 us
    pallas_call x1, Pallas kernels, carried(): pl.pallas_call(functools.partial(carry_kernel, pieces, rows), in_specs=[v...  23.7 us
    pallas_call x1, Pallas kernels, on_device(): pl.pallas_call(functools.partial(first_kernel, members), grid=(chans // w...  23.3 us
    pallas_call x1, Pallas kernels, summed(): pl.pallas_call(sum_kernel, in_specs=[vmem], out_specs=vmem, out_shape=jax...  20.6 us
    ppermute x2, waiting for transfers between devices, moved(): lax.ppermute(block, LINE, [(i, i + distance) for i in devices if i + dist...  8.69 us
    ppermute x2, starting transfers between devices, moved(): lax.ppermute(block, LINE, [(i, i + distance) for i in devices if i + dist...  6.77 us
  transfers between devices with their start and end apart: 2, of which 1 were waited for; matrix products, arithmetic and copies ran while one was open for 0% of the time, Pallas kernels for 0%

profile of v2, /device:TPU:0, one launch (start us, length us, event | category | flops | bytes accessed | tf_op | source)
XLA Modules:
  0.0 133.5 jit_solution(11122688339770947051)
XLA Ops:
  0.6 0.0 copy-start
  0.6 0.0 copy-start.2
  0.7 0.0 copy-start.1
  0.7 0.0 copy-start.3
  0.7 0.0 copy-start.5
  0.7 0.0 copy-start.4
  0.7 1.1 slice_bitcast_fusion.4
  1.8 1.0 slice_bitcast_fusion.2
  2.8 1.3 collective-permute-start.1
  4.2 5.5 %collective-permute-start = (bf16[3,8,4096]{2,1,0:T(8,128)(2,1)S(1)}, bf16[3,8,4096]{2,1,0:T(8,128)(2,1)S(1)}, u32[]{:S(2)}, u32[]{:S(2)}) collective-permute-start(bf16[3,8,4096]{2,1,0:T(8,128)(2,1)S(1)} %pad_maximum_fusion.2), channel_id=1, source_target_pairs={{0,2},{2,4},{4,6},{6,8},{8,10},{10,12},{12,14},{1,3},{3,5},{5,7},{... | collective-permute-start | bytes 589832 | tf_op jit(solution)/shard_map/ppermute | solution.py:21
  9.6 8.7 %collective-permute-done = bf16[3,8,4096]{2,1,0:T(8,128)(2,1)S(1)} collective-permute-done((bf16[3,8,4096]{2,1,0:T(8,128)(2,1)S(1)}, bf16[3,8,4096]{2,1,0:T(8,128)(2,1)S(1)}, u32[]{:S(2)}, u32[]{:S(2)}) %collective-permute-start) | collective-permute-done | bytes 196640 | tf_op jit(solution)/shard_map/ppermute | solution.py:21
  18.4 0.0 collective-permute-done.1
  18.5 0.0 copy-done
  18.5 0.0 copy-done.2
  18.5 0.0 copy-done.1
  18.5 0.0 copy-done.3
  18.5 0.0 copy-done.5
  18.5 0.0 copy-done.4
  18.5 23.3 %local_states.1 = (f32[3,136,4096]{2,1,0:T(8,128)}, f32[16,8,4096]{2,1,0:T(8,128)}, f32[16,8,4096]{2,1,0:T(8,128)}, f32[16,4096]{1,0:T(8,128)S(1)}, f32[16,4096]...) custom-call(bf16[128,4096]{1,0:T(8,128)(2,1)S(1)} %copy-done, bf16[128,4096]{1,0:T(8,128)(2,1)S(1)} %copy-done.1, ...), custom_call_target="tpu_custom_call" | custom-call | tf_op jit(solution)/shard_map/local_states/pallas_call | solution.py:473
  41.8 23.7 %carry.1 = (f32[16,4096]{1,0:T(8,128)S(1)}, f32[16,4096]{1,0:T(8,128)S(1)}) custom-call(f32[16,4096]{1,0:T(8,128)S(1)} %get-tuple-element.24.final_ref, f32[16,4096]{1,0:T(8,128)S(1)} %get-tuple-element.27.first_ref, f32[16,4096]{1,0:T(8,128)S(1)} %get-tuple-element.25.rates_ref), custom_call_target="tpu_custom_call" | custom-call | tf_op jit(solution)/shard_map/carry/pallas_call | solution.py:161
  65.6 45.8 %gradients.1 = (bf16[128,4096]{1,0:T(8,128)(2,1)}, bf16[128,4096]{1,0:T(8,128)(2,1)}, bf16[128,4096]{1,0:T(8,128)(2,1)}, f32[3,8,4096]{2,1,0:T(8,128)S(1)}, f32[...) custom-call(bf16[128,4096]{1,0:T(8,128)(2,1)S(1)} %copy-done, bf16[128,4096]{1,0:T(8,128)(2,1)S(1)} %copy-done.1, ...), custom_call_target="tpu_custom_call" | custom-call | tf_op jit(solution)/shard_map/gradients/pallas_call | solution.py:492
  111.5 20.6 %sums.1 = f32[8,104,128]{2,1,0:T(8,128)S(1)} custom-call(f32[8,104,128]{2,1,0:T(8,128)S(1)} %bitcast.50), custom_call_target="tpu_custom_call" | custom-call | tf_op jit(solution)/shard_map/sums/pallas_call | solution.py:229
  132.0 0.6 slice_multiply_fusion.1
  132.7 0.8 slice_multiply_fusion
  (8 shorter events, 0.2 us)
Async XLA Ops:
  0.6 17.8 %copy-start = (bf16[128,4096]{1,0:T(8,128)(2,1)S(1)}, bf16[128,4096]{1,0:T(8,128)(2,1)}, u32[]{:S(2)}) copy-start(bf16[128,4096]{1,0:T(8,128)(2,1)} %q_ref.3) | copy-start | bytes 3145732
  0.6 17.8 %copy-start.2 = (bf16[128,4096]{1,0:T(8,128)(2,1)S(1)}, bf16[128,4096]{1,0:T(8,128)(2,1)}, u32[]{:S(2)}) copy-start(bf16[128,4096]{1,0:T(8,128)(2,1)} %v_ref.3) | copy-start | bytes 3145732
  0.7 17.8 %copy-start.1 = (bf16[128,4096]{1,0:T(8,128)(2,1)S(1)}, bf16[128,4096]{1,0:T(8,128)(2,1)}, u32[]{:S(2)}) copy-start(bf16[128,4096]{1,0:T(8,128)(2,1)} %k_ref.3) | copy-start | bytes 3145732
  0.7 17.8 %copy-start.3 = (f32[3,7,4096]{2,1,0:T(8,128)S(1)}, f32[3,7,4096]{2,1,0:T(8,128)}, u32[]{:S(2)}) copy-start(f32[3,7,4096]{2,1,0:T(8,128)} %taps_ref.3) | copy-start | bytes 1032196
  0.7 17.8 %copy-start.5 = (f32[16,256]{1,0:T(8,128)S(1)}, f32[16,256]{1,0:T(8,128)}, u32[]{:S(2)}) copy-start(f32[16,256]{1,0:T(8,128)} %res_ref.1) | copy-start | bytes 49156
  0.7 17.8 %copy-start.4 = (f32[16,256]{1,0:T(8,128)S(1)}, f32[16,256]{1,0:T(8,128)}, u32[]{:S(2)}) copy-start(f32[16,256]{1,0:T(8,128)} %rate_ref.1) | copy-start | bytes 49156
  2.8 15.5 %collective-permute-start.1 = (bf16[4,8,4096]{2,1,0:T(8,128)(2,1)S(1)}, bf16[4,8,4096]{2,1,0:T(8,128)(2,1)S(1)}, u32[]{:S(2)}, u32[]{:S(2)}) collective-permute-start(bf16[4,8,4096]{2,1,0:T(8,128)(2,1)S(1)} %pad_maximum_fusion.1), channel_id=1, source_target_pairs={{2,0},{4,2},{6,4},{8,6},{10,8},{12,10},{14,12},{3,1},{5,3},{7,5},{... | collective-permute-start | bytes 786440 | tf_op jit(solution)/shard_map/ppermute | solution.py:21
  4.2 14.2 %collective-permute-start = (bf16[3,8,4096]{2,1,0:T(8,128)(2,1)S(1)}, bf16[3,8,4096]{2,1,0:T(8,128)(2,1)S(1)}, u32[]{:S(2)}, u32[]{:S(2)}) collective-permute-start(bf16[3,8,4096]{2,1,0:T(8,128)(2,1)S(1)} %pad_maximum_fusion.2), channel_id=1, source_target_pairs={{0,2},{2,4},{4,6},{6,8},{8,10},{10,12},{12,14},{1,3},{3,5},{5,7},{... | collective-permute-start | bytes 589832 | tf_op jit(solution)/shard_map/ppermute | solution.py:21

commit v3 on v2

--- a/solution.py
+++ b/solution.py
@@ -10,10 +10,9 @@
 LINE = ("ctx", "inner")
 LANES = 128
 SUB = 8
-TOGETHER = 4
+TOGETHER = 8
 PIECE = 1024
 MESH = pl.DeviceIdType.MESH
-EXACT = lax.Precision.HIGHEST
 
 
 def moved(block, distance):
@@ -253,12 +252,24 @@
     return flat.reshape(lead, chans // LANES, sub, LANES).transpose(0, 2, 1, 3).reshape(lead, sub, chans)
 
 
-def spread_matrix(local_groups, width, members):
-    first = pl.program_id(0) * width
-    row = lax.broadcasted_iota(jnp.int32, (local_groups, width), 0)
-    col = lax.broadcasted_iota(jnp.int32, (local_groups, width), 1) + first
-    low = row * members
-    return jnp.where((col >= low) & (col < low + members), 1.0, 0.0).astype(jnp.float32)
+def spread_matrix(local_groups, width, members, over_rows):
+    shape = (width, local_groups) if over_rows else (local_groups, width)
+    chan = lax.broadcasted_iota(jnp.int32, shape, 0 if over_rows else 1) + pl.program_id(0) * width
+    low = lax.broadcasted_iota(jnp.int32, shape, 1 if over_rows else 0) * members
+    return jnp.where((chan >= low) & (chan < low + members), 1.0, 0.0).astype(jnp.bfloat16)
+
+
+def table_dots(tables, onto):
+    terms = []
+    for rest in tables:
+        for _ in range(3):
+            term = rest.astype(jnp.bfloat16)
+            terms.append(term)
+            rest = rest - term.astype(jnp.float32)
+    rows = tables[0].shape[0]
+    out = jnp.dot(jnp.concatenate(terms, axis=0), onto, preferred_element_type=jnp.float32)
+    cut = [out[i * rows:(i + 1) * rows] for i in range(len(terms))]
+    return [cut[3 * i] + cut[3 * i + 1] + cut[3 * i + 2] for i in range(len(tables))]
 
 
 def first_kernel(members, q_ref, k_ref, v_ref, g_ref, prev_ref, next_ref, taps_ref, rate_ref, res_ref,
@@ -267,9 +278,8 @@
     modes, local_groups = rate_ref.shape
     tap_count = taps_ref.shape[1]
     steps = rows // SUB
-    onto = spread_matrix(local_groups, width, members)
-    rates_ref[...] = jnp.dot(rate_ref[...], onto, precision=EXACT, preferred_element_type=jnp.float32)
-    ress_ref[...] = jnp.dot(res_ref[...], onto, precision=EXACT, preferred_element_type=jnp.float32)
+    onto = spread_matrix(local_groups, width, members, False)
+    rates_ref[...], ress_ref[...] = table_dots([rate_ref[...], res_ref[...]], onto)
     for i, x_ref in enumerate((q_ref, k_ref, v_ref)):
         wide[i, 0:SUB] = prev_ref[i]
         wide[i, SUB:SUB + rows] = x_ref[...].astype(jnp.float32)
@@ -427,20 +437,16 @@
             for j in range(tap_count, SUB):
                 tap_ref[i, j:j + 1, cols] = jnp.zeros((1, LANES), jnp.float32)
 
-    onto = spread_matrix(local_groups, width, members)
-    along = (((1,), (1,)), ((), ()))
+    onto = spread_matrix(local_groups, width, members, True)
+    mode_part, pole_part = table_dots([mode_rows[...], pole_rows[...]], onto)
 
     @pl.when(pl.program_id(0) == 0)
     def _():
         mode_ref[...] = jnp.zeros_like(mode_ref)
         pole_ref[...] = jnp.zeros_like(pole_ref)
 
-    mode_ref[...] += lax.dot_general(
-        mode_rows[...], onto, along, precision=EXACT, preferred_element_type=jnp.float32
-    )
-    pole_ref[...] += lax.dot_general(
-        pole_rows[...], onto, along, precision=EXACT, preferred_element_type=jnp.float32
-    )
+    mode_ref[...] += mode_part
+    pole_ref[...] += pole_part
 
 
 def on_device(queries, keys_in, values_in, out_grad, short_taps, pole_rate, residue):

time: 134 us -> 124 us (0.925)
  Pallas kernels: 113 us -> 104 us
    pallas_call x1, Pallas kernels: 45.8 us -> 39.8 us  [on_device(): pl.pallas_call(functools.partial(second_kernel, members), grid=(chans //...]
    pallas_call x1, Pallas kernels: 23.3 us -> 19.9 us  [on_device(): pl.pallas_call(functools.partial(first_kernel, members), grid=(chans // w...]
where the time goes in v3:
time: 124 us
  Pallas kernels  104 us (84%)
  waiting for transfers between devices  8.69 us (7%)
  starting transfers between devices  6.77 us (5%)
  local copies, waits for them, and re-layouts  2.17 us (2%)
  other arithmetic  1.54 us (1%)
    pallas_call x1, Pallas kernels, on_device(): pl.pallas_call(functools.partial(second_kernel, members), grid=(chans //...  39.8 us
    pallas_call x1, Pallas kernels, carried(): pl.pallas_call(functools.partial(carry_kernel, pieces, rows), in_specs=[v...  23.7 us
    pallas_call x1, Pallas kernels, summed(): pl.pallas_call(sum_kernel, in_specs=[vmem], out_specs=vmem, out_shape=jax...  20.6 us
    pallas_call x1, Pallas kernels, on_device(): pl.pallas_call(functools.partial(first_kernel, members), grid=(chans // w...  19.9 us
    ppermute x2, waiting for transfers between devices, moved(): lax.ppermute(block, LINE, [(i, i + distance) for i in devices if i + dist...  8.69 us
    ppermute x2, starting transfers between devices, moved(): lax.ppermute(block, LINE, [(i, i + distance) for i in devices if i + dist...  6.77 us
  transfers between devices with their start and end apart: 2, of which 1 were waited for; matrix products, arithmetic and copies ran while one was open for 0% of the time, Pallas kernels for 0%

profile of v3, /device:TPU:0, one launch (start us, length us, event | category | flops | bytes accessed | tf_op | source)
XLA Modules:
  0.0 124.0 jit_solution(6726218122108032339)
XLA Ops:
  0.6 0.0 copy-start
  0.6 0.0 copy-start.2
  0.7 0.0 copy-start.1
  0.7 0.0 copy-start.3
  0.7 0.0 copy-start.5
  0.7 0.0 copy-start.4
  0.7 1.1 slice_bitcast_fusion.4
  1.8 1.0 slice_bitcast_fusion.2
  2.8 1.3 %collective-permute-start.1 = (bf16[4,8,4096]{2,1,0:T(8,128)(2,1)S(1)}, bf16[4,8,4096]{2,1,0:T(8,128)(2,1)S(1)}, u32[]{:S(2)}, u32[]{:S(2)}) collective-permute-start(bf16[4,8,4096]{2,1,0:T(8,128)(2,1)S(1)} %pad_maximum_fusion.1), channel_id=1, source_target_pairs={{2,0},{4,2},{6,4},{8,6},{10,8},{12,10},{14,12},{3,1},{5,3},{7,5},{... | collective-permute-start | bytes 786440 | tf_op jit(solution)/shard_map/ppermute | solution.py:20
  4.2 5.5 %collective-permute-start = (bf16[3,8,4096]{2,1,0:T(8,128)(2,1)S(1)}, bf16[3,8,4096]{2,1,0:T(8,128)(2,1)S(1)}, u32[]{:S(2)}, u32[]{:S(2)}) collective-permute-start(bf16[3,8,4096]{2,1,0:T(8,128)(2,1)S(1)} %pad_maximum_fusion.2), channel_id=1, source_target_pairs={{0,2},{2,4},{4,6},{6,8},{8,10},{10,12},{12,14},{1,3},{3,5},{5,7},{... | collective-permute-start | bytes 589832 | tf_op jit(solution)/shard_map/ppermute | solution.py:20
  9.6 8.7 %collective-permute-done = bf16[3,8,4096]{2,1,0:T(8,128)(2,1)S(1)} collective-permute-done((bf16[3,8,4096]{2,1,0:T(8,128)(2,1)S(1)}, bf16[3,8,4096]{2,1,0:T(8,128)(2,1)S(1)}, u32[]{:S(2)}, u32[]{:S(2)}) %collective-permute-start) | collective-permute-done | bytes 196640 | tf_op jit(solution)/shard_map/ppermute | solution.py:20
  18.4 0.0 collective-permute-done.1
  18.5 0.0 copy-done
  18.5 0.0 copy-done.2
  18.5 0.0 copy-done.1
  18.5 0.0 copy-done.3
  18.5 0.0 copy-done.5
  18.5 0.0 copy-done.4
  18.5 19.9 %local_states.1 = (f32[3,136,4096]{2,1,0:T(8,128)}, f32[16,8,4096]{2,1,0:T(8,128)}, f32[16,8,4096]{2,1,0:T(8,128)}, f32[16,4096]{1,0:T(8,128)S(1)}, f32[16,4096]...) custom-call(bf16[128,4096]{1,0:T(8,128)(2,1)S(1)} %copy-done, bf16[128,4096]{1,0:T(8,128)(2,1)S(1)} %copy-done.1, ...), custom_call_target="tpu_custom_call" | custom-call | tf_op jit(solution)/shard_map/local_states/pallas_call | solution.py:479
  38.4 23.7 %carry.1 = (f32[16,4096]{1,0:T(8,128)S(1)}, f32[16,4096]{1,0:T(8,128)S(1)}) custom-call(f32[16,4096]{1,0:T(8,128)S(1)} %get-tuple-element.24.final_ref, f32[16,4096]{1,0:T(8,128)S(1)} %get-tuple-element.27.first_ref, f32[16,4096]{1,0:T(8,128)S(1)} %get-tuple-element.25.rates_ref), custom_call_target="tpu_custom_call" | custom-call | tf_op jit(solution)/shard_map/carry/pallas_call | solution.py:160
  62.1 39.8 %gradients.1 = (bf16[128,4096]{1,0:T(8,128)(2,1)}, bf16[128,4096]{1,0:T(8,128)(2,1)}, bf16[128,4096]{1,0:T(8,128)(2,1)}, f32[3,8,4096]{2,1,0:T(8,128)S(1)}, f32[...) custom-call(bf16[128,4096]{1,0:T(8,128)(2,1)S(1)} %copy-done, bf16[128,4096]{1,0:T(8,128)(2,1)S(1)} %copy-done.1, ...), custom_call_target="tpu_custom_call" | custom-call | tf_op jit(solution)/shard_map/gradients/pallas_call | solution.py:498
  102.0 20.6 %sums.1 = f32[8,104,128]{2,1,0:T(8,128)S(1)} custom-call(f32[8,104,128]{2,1,0:T(8,128)S(1)} %bitcast.50), custom_call_target="tpu_custom_call" | custom-call | tf_op jit(solution)/shard_map/sums/pallas_call | solution.py:228
  122.6 0.6 slice_multiply_fusion.1
  123.2 0.8 slice_multiply_fusion
  (8 shorter events, 0.2 us)
Async XLA Ops:
  0.6 17.8 %copy-start = (bf16[128,4096]{1,0:T(8,128)(2,1)S(1)}, bf16[128,4096]{1,0:T(8,128)(2,1)}, u32[]{:S(2)}) copy-start(bf16[128,4096]{1,0:T(8,128)(2,1)} %q_ref.3) | copy-start | bytes 3145732
  0.6 17.8 %copy-start.2 = (bf16[128,4096]{1,0:T(8,128)(2,1)S(1)}, bf16[128,4096]{1,0:T(8,128)(2,1)}, u32[]{:S(2)}) copy-start(bf16[128,4096]{1,0:T(8,128)(2,1)} %v_ref.3) | copy-start | bytes 3145732
  0.7 17.8 %copy-start.1 = (bf16[128,4096]{1,0:T(8,128)(2,1)S(1)}, bf16[128,4096]{1,0:T(8,128)(2,1)}, u32[]{:S(2)}) copy-start(bf16[128,4096]{1,0:T(8,128)(2,1)} %k_ref.3) | copy-start | bytes 3145732
  0.7 17.8 %copy-start.3 = (f32[3,7,4096]{2,1,0:T(8,128)S(1)}, f32[3,7,4096]{2,1,0:T(8,128)}, u32[]{:S(2)}) copy-start(f32[3,7,4096]{2,1,0:T(8,128)} %taps_ref.3) | copy-start | bytes 1032196
  0.7 17.8 %copy-start.5 = (f32[16,256]{1,0:T(8,128)S(1)}, f32[16,256]{1,0:T(8,128)}, u32[]{:S(2)}) copy-start(f32[16,256]{1,0:T(8,128)} %res_ref.1) | copy-start | bytes 49156
  0.7 17.8 %copy-start.4 = (f32[16,256]{1,0:T(8,128)S(1)}, f32[16,256]{1,0:T(8,128)}, u32[]{:S(2)}) copy-start(f32[16,256]{1,0:T(8,128)} %rate_ref.1) | copy-start | bytes 49156
  2.8 15.5 %collective-permute-start.1 = (bf16[4,8,4096]{2,1,0:T(8,128)(2,1)S(1)}, bf16[4,8,4096]{2,1,0:T(8,128)(2,1)S(1)}, u32[]{:S(2)}, u32[]{:S(2)}) collective-permute-start(bf16[4,8,4096]{2,1,0:T(8,128)(2,1)S(1)} %pad_maximum_fusion.1), channel_id=1, source_target_pairs={{2,0},{4,2},{6,4},{8,6},{10,8},{12,10},{14,12},{3,1},{5,3},{7,5},{... | collective-permute-start | bytes 786440 | tf_op jit(solution)/shard_map/ppermute | solution.py:20
  4.2 14.2 %collective-permute-start = (bf16[3,8,4096]{2,1,0:T(8,128)(2,1)S(1)}, bf16[3,8,4096]{2,1,0:T(8,128)(2,1)S(1)}, u32[]{:S(2)}, u32[]{:S(2)}) collective-permute-start(bf16[3,8,4096]{2,1,0:T(8,128)(2,1)S(1)} %pad_maximum_fusion.2), channel_id=1, source_target_pairs={{0,2},{2,4},{4,6},{6,8},{8,10},{10,12},{12,14},{1,3},{3,5},{5,7},{... | collective-permute-start | bytes 589832 | tf_op jit(solution)/shard_map/ppermute | solution.py:20

commit v4 on v3

--- a/solution.py
+++ b/solution.py
@@ -11,7 +11,7 @@
 LANES = 128
 SUB = 8
 TOGETHER = 8
-PIECE = 1024
+PIECE = 512
 MESH = pl.DeviceIdType.MESH
 
 

time: 124 us -> 122 us (0.984)
  Pallas kernels: 104 us -> 102 us
    pallas_call x1, Pallas kernels: 23.7 us -> 22.1 us  [carried(): pl.pallas_call(functools.partial(carry_kernel, pieces, rows), in_specs=[v...]
where the time goes in v4:
time: 122 us
  Pallas kernels  102 us (84%)
  waiting for transfers between devices  8.69 us (7%)
  starting transfers between devices  6.77 us (6%)
  local copies, waits for them, and re-layouts  2.17 us (2%)
  other arithmetic  1.54 us (1%)
    pallas_call x1, Pallas kernels, on_device(): pl.pallas_call(functools.partial(second_kernel, members), grid=(chans //...  39.8 us
    pallas_call x1, Pallas kernels, carried(): pl.pallas_call(functools.partial(carry_kernel, pieces, rows), in_specs=[v...  22.1 us
    pallas_call x1, Pallas kernels, summed(): pl.pallas_call(sum_kernel, in_specs=[vmem], out_specs=vmem, out_shape=jax...  20.5 us
    pallas_call x1, Pallas kernels, on_device(): pl.pallas_call(functools.partial(first_kernel, members), grid=(chans // w...  19.9 us
    ppermute x2, waiting for transfers between devices, moved(): lax.ppermute(block, LINE, [(i, i + distance) for i in devices if i + dist...  8.69 us
    ppermute x2, starting transfers between devices, moved(): lax.ppermute(block, LINE, [(i, i + distance) for i in devices if i + dist...  6.77 us
  transfers between devices with their start and end apart: 2, of which 1 were waited for; matrix products, arithmetic and copies ran while one was open for 0% of the time, Pallas kernels for 0%

profile of v4, /device:TPU:0, one launch (start us, length us, event | category | flops | bytes accessed | tf_op | source)
XLA Modules:
  0.0 122.3 jit_solution(12940770613328060011)
XLA Ops:
  0.6 0.0 copy-start
  0.6 0.0 copy-start.2
  0.7 0.0 copy-start.1
  0.7 0.0 copy-start.3
  0.7 0.0 copy-start.5
  0.7 0.0 copy-start.4
  0.7 1.1 slice_bitcast_fusion.4
  1.8 1.0 slice_bitcast_fusion.2
  2.8 1.3 %collective-permute-start.1 = (bf16[4,8,4096]{2,1,0:T(8,128)(2,1)S(1)}, bf16[4,8,4096]{2,1,0:T(8,128)(2,1)S(1)}, u32[]{:S(2)}, u32[]{:S(2)}) collective-permute-start(bf16[4,8,4096]{2,1,0:T(8,128)(2,1)S(1)} %pad_maximum_fusion.1), channel_id=1, source_target_pairs={{2,0},{4,2},{6,4},{8,6},{10,8},{12,10},{14,12},{3,1},{5,3},{7,5},{... | collective-permute-start | bytes 786440 | tf_op jit(solution)/shard_map/ppermute | solution.py:20
  4.2 5.5 %collective-permute-start = (bf16[3,8,4096]{2,1,0:T(8,128)(2,1)S(1)}, bf16[3,8,4096]{2,1,0:T(8,128)(2,1)S(1)}, u32[]{:S(2)}, u32[]{:S(2)}) collective-permute-start(bf16[3,8,4096]{2,1,0:T(8,128)(2,1)S(1)} %pad_maximum_fusion.2), channel_id=1, source_target_pairs={{0,2},{2,4},{4,6},{6,8},{8,10},{10,12},{12,14},{1,3},{3,5},{5,7},{... | collective-permute-start | bytes 589832 | tf_op jit(solution)/shard_map/ppermute | solution.py:20
  9.6 8.7 %collective-permute-done = bf16[3,8,4096]{2,1,0:T(8,128)(2,1)S(1)} collective-permute-done((bf16[3,8,4096]{2,1,0:T(8,128)(2,1)S(1)}, bf16[3,8,4096]{2,1,0:T(8,128)(2,1)S(1)}, u32[]{:S(2)}, u32[]{:S(2)}) %collective-permute-start) | collective-permute-done | bytes 196640 | tf_op jit(solution)/shard_map/ppermute | solution.py:20
  18.4 0.0 collective-permute-done.1
  18.5 0.0 copy-done
  18.5 0.0 copy-done.2
  18.5 0.0 copy-done.1
  18.5 0.0 copy-done.3
  18.5 0.0 copy-done.5
  18.5 0.0 copy-done.4
  18.5 19.9 %local_states.1 = (f32[3,136,4096]{2,1,0:T(8,128)}, f32[16,8,4096]{2,1,0:T(8,128)}, f32[16,8,4096]{2,1,0:T(8,128)}, f32[16,4096]{1,0:T(8,128)S(1)}, f32[16,4096]...) custom-call(bf16[128,4096]{1,0:T(8,128)(2,1)S(1)} %copy-done, bf16[128,4096]{1,0:T(8,128)(2,1)S(1)} %copy-done.1, ...), custom_call_target="tpu_custom_call" | custom-call | tf_op jit(solution)/shard_map/local_states/pallas_call | solution.py:479
  38.4 22.1 %carry.1 = (f32[16,4096]{1,0:T(8,128)S(1)}, f32[16,4096]{1,0:T(8,128)S(1)}) custom-call(f32[16,4096]{1,0:T(8,128)S(1)} %get-tuple-element.24.final_ref, f32[16,4096]{1,0:T(8,128)S(1)} %get-tuple-element.27.first_ref, f32[16,4096]{1,0:T(8,128)S(1)} %get-tuple-element.25.rates_ref), custom_call_target="tpu_custom_call" | custom-call | tf_op jit(solution)/shard_map/carry/pallas_call | solution.py:160
  60.5 39.8 %gradients.1 = (bf16[128,4096]{1,0:T(8,128)(2,1)}, bf16[128,4096]{1,0:T(8,128)(2,1)}, bf16[128,4096]{1,0:T(8,128)(2,1)}, f32[3,8,4096]{2,1,0:T(8,128)S(1)}, f32[...) custom-call(bf16[128,4096]{1,0:T(8,128)(2,1)S(1)} %copy-done, bf16[128,4096]{1,0:T(8,128)(2,1)S(1)} %copy-done.1, ...), custom_call_target="tpu_custom_call" | custom-call | tf_op jit(solution)/shard_map/gradients/pallas_call | solution.py:498
  100.3 20.5 %sums.1 = f32[8,104,128]{2,1,0:T(8,128)S(1)} custom-call(f32[8,104,128]{2,1,0:T(8,128)S(1)} %bitcast.50), custom_call_target="tpu_custom_call" | custom-call | tf_op jit(solution)/shard_map/sums/pallas_call | solution.py:228
  120.9 0.6 slice_multiply_fusion.1
  121.5 0.8 slice_multiply_fusion
  (8 shorter events, 0.2 us)
Async XLA Ops:
  0.6 17.8 %copy-start = (bf16[128,4096]{1,0:T(8,128)(2,1)S(1)}, bf16[128,4096]{1,0:T(8,128)(2,1)}, u32[]{:S(2)}) copy-start(bf16[128,4096]{1,0:T(8,128)(2,1)} %q_ref.3) | copy-start | bytes 3145732
  0.6 17.8 %copy-start.2 = (bf16[128,4096]{1,0:T(8,128)(2,1)S(1)}, bf16[128,4096]{1,0:T(8,128)(2,1)}, u32[]{:S(2)}) copy-start(bf16[128,4096]{1,0:T(8,128)(2,1)} %v_ref.3) | copy-start | bytes 3145732
  0.7 17.8 %copy-start.1 = (bf16[128,4096]{1,0:T(8,128)(2,1)S(1)}, bf16[128,4096]{1,0:T(8,128)(2,1)}, u32[]{:S(2)}) copy-start(bf16[128,4096]{1,0:T(8,128)(2,1)} %k_ref.3) | copy-start | bytes 3145732
  0.7 17.8 %copy-start.3 = (f32[3,7,4096]{2,1,0:T(8,128)S(1)}, f32[3,7,4096]{2,1,0:T(8,128)}, u32[]{:S(2)}) copy-start(f32[3,7,4096]{2,1,0:T(8,128)} %taps_ref.3) | copy-start | bytes 1032196
  0.7 17.8 %copy-start.5 = (f32[16,256]{1,0:T(8,128)S(1)}, f32[16,256]{1,0:T(8,128)}, u32[]{:S(2)}) copy-start(f32[16,256]{1,0:T(8,128)} %res_ref.1) | copy-start | bytes 49156
  0.7 17.8 %copy-start.4 = (f32[16,256]{1,0:T(8,128)S(1)}, f32[16,256]{1,0:T(8,128)}, u32[]{:S(2)}) copy-start(f32[16,256]{1,0:T(8,128)} %rate_ref.1) | copy-start | bytes 49156
  2.8 15.5 %collective-permute-start.1 = (bf16[4,8,4096]{2,1,0:T(8,128)(2,1)S(1)}, bf16[4,8,4096]{2,1,0:T(8,128)(2,1)S(1)}, u32[]{:S(2)}, u32[]{:S(2)}) collective-permute-start(bf16[4,8,4096]{2,1,0:T(8,128)(2,1)S(1)} %pad_maximum_fusion.1), channel_id=1, source_target_pairs={{2,0},{4,2},{6,4},{8,6},{10,8},{12,10},{14,12},{3,1},{5,3},{7,5},{... | collective-permute-start | bytes 786440 | tf_op jit(solution)/shard_map/ppermute | solution.py:20
  4.2 14.2 %collective-permute-start = (bf16[3,8,4096]{2,1,0:T(8,128)(2,1)S(1)}, bf16[3,8,4096]{2,1,0:T(8,128)(2,1)S(1)}, u32[]{:S(2)}, u32[]{:S(2)}) collective-permute-start(bf16[3,8,4096]{2,1,0:T(8,128)(2,1)S(1)} %pad_maximum_fusion.2), channel_id=1, source_target_pairs={{0,2},{2,4},{4,6},{6,8},{8,10},{10,12},{12,14},{1,3},{3,5},{5,7},{... | collective-permute-start | bytes 589832 | tf_op jit(solution)/shard_map/ppermute | solution.py:20
